TPU v7x, 512 devices: a whole 4x4x16 slice. The times are simulated.
512 devices in a mesh: seq: 16 (over z), exp: 32 (over x, y, core).
Axes of the slice: x: 4, y: 4, z: 16, core: 2. Of those that a mesh axis runs over, the one named last changes fastest.
Arguments:
- patches: bfloat16 [32, 3584, 3072], P('exp', 'seq'), may hold values from -8 to 8
- slot_keys: bfloat16 [32, 3072], P('exp'), may hold values from -0.05593081 to 0.05593081
- w_in: bfloat16 [32, 3072, 3072], P('exp', None, 'seq'), may hold values from -0.109375 to 0.109375
- w_out: bfloat16 [32, 3072, 3072], P('exp', 'seq'), may hold values from -0.21875 to 0.21875
Outputs:
- mixed: bfloat16 [32, 3584, 3072], P('exp', 'seq')
All inputs are finite; a program needn't handle non-finite values.
Results may differ from a plain program's by a relative error of at most 0.0071.
Values may be sent and summed in bfloat16 or wider, within the bound.
No kernel may reach another device: no remote copies, remote signals or barrier semaphores. Data moves between devices by JAX's collectives and lax.ppermute only.
A program may use at most 64 MiB of HBM per device.

v0:
```python
import jax
import jax.numpy as jnp
from jax import lax
from jax.sharding import PartitionSpec as P


def shards(patches, slot_keys, w_in, w_out):
    patch_rows = patches[0]
    first_proj = w_in[0]
    second_proj = w_out[0]
    slot_table = lax.all_gather(slot_keys, "exp", axis=0, tiled=True)
    logits = lax.dot_general(
        patch_rows, slot_table, (((1,), (1,)), ((), ())), preferred_element_type=jnp.float32
    )
    combine = jax.nn.softmax(logits, axis=1).astype(jnp.bfloat16)
    local_max = jnp.max(logits, axis=0)
    column_max = lax.pmax(local_max, "seq")
    raised = jnp.exp(logits - column_max[None, :])
    dispatch = raised.astype(jnp.bfloat16)
    part_sum = jnp.sum(raised, axis=0)
    partial_value = lax.dot_general(
        dispatch, patch_rows, (((0,), (0,)), ((), ())), preferred_element_type=jnp.float32
    )
    total, denom = lax.psum((partial_value, part_sum), "seq")
    slot_in = (total / denom[:, None]).astype(jnp.bfloat16)
    owned = lax.all_to_all(slot_in, "exp", split_axis=0, concat_axis=0, tiled=True)
    hidden = jnp.dot(owned, first_proj, preferred_element_type=jnp.float32)
    activated = jax.nn.gelu(hidden).astype(jnp.bfloat16)
    out_term = jnp.dot(activated, second_proj, preferred_element_type=jnp.float32)
    out_whole = lax.psum(out_term, "seq").astype(jnp.bfloat16)
    returned = lax.all_to_all(out_whole, "exp", split_axis=0, concat_axis=0, tiled=True)
    mixed = jnp.dot(combine, returned, preferred_element_type=jnp.float32)
    return mixed.astype(jnp.bfloat16)[None]


def solution(mesh):
    placed = (P("exp", "seq", None), P("exp", None), P("exp", None, "seq"), P("exp", "seq", None))
    return jax.shard_map(
        shards, mesh=mesh, in_specs=placed, out_specs=P("exp", "seq", None), check_vma=False
    )
```

profile of v0, /device:TPU:1, one launch (start us, length us, event | category | flops | bytes accessed | tf_op | source)
XLA Modules:
  0.0 302.1 jit_solution(11859119506205627683)
XLA Ops:
  6.5 0.0 copy-start
  6.5 0.0 all-reduce.3.cloned.1.call-start
  6.5 29.3 %all-gather = bf16[32,1,3072]{2,1,0:T(2,128)(2,1)S(1)} all-gather(bf16[1,1,3072]{2,1,0:T(2,128)(2,1)} %bitcast.45), channel_id=1, replica_groups=mesh['seq'=16,'exp'=32] {'exp'}, dimensions={0}, use_global_device_ids=true | all-gather | bytes 202752 | tf_op jit(solution)/shard_map/all_gather | solution.py:11
  35.9 0.0 copy-done
  35.9 0.6 fusion.51
  36.5 26.5 %pmax.7 = f32[32]{0:T(128)S(1)} all-reduce(f32[32]{0:T(128)S(1)} %get-tuple-element.8), channel_id=1, replica_groups=mesh['seq'=16,'exp'=32] {'seq'}, use_global_device_ids=true, to_apply=%region_3.0 | all-reduce | flops 32 | bytes 256 | tf_op jit(solution)/shard_map/pmax | solution.py:17
  63.0 1.2 fusion.1
  64.2 0.0 copy-start.1
  64.2 0.0 all-reduce.3.cloned.1.call-update
  64.2 0.2 fusion.36
  64.4 20.5 %psum.22 = f32[32]{0:T(128)S(1)} all-reduce(f32[32]{0:T(128)S(1)} %get-tuple-element.6), channel_id=1, replica_groups=mesh['seq'=16,'exp'=32] {'seq'}, use_global_device_ids=true, to_apply=%region_6.0 | all-reduce | flops 32 | bytes 256 | tf_op jit(solution)/shard_map/psum | solution.py:24
  84.9 106.8 %all-reduce.3.cloned.1.call-done = f32[32,3072]{1,0:T(8,128)} async-done(((f32[32,3072]{1,0:T(8,128)}), f32[32,3072]{1,0:T(8,128)}) %all-reduce.3.cloned.1.call-update) | async-done | bytes 393232 | tf_op jit(solution)/shard_map/psum | solution.py:24
  191.7 1.1 fusion.15
  192.8 0.5 broadcast.4
  193.4 0.7 reduce
  194.1 0.1 reshape.10
  194.2 25.1 %all_to_all.24 = bf16[32,2,1536]{2,1,0:T(2,128)(2,1)S(1)} all-to-all(bf16[32,2,1536]{2,1,0:T(2,128)(2,1)S(1)} %reshape.10), channel_id=1, replica_groups=mesh['seq'=16,'exp'=32] {'exp'}, dimensions={0} | all-to-all | bytes 393216 | tf_op jit(solution)/shard_map/all_to_all | solution.py:26
  219.3 0.1 reshape.11
  219.4 0.0 copy-done.1
  219.4 2.2 fusion.5
  221.7 45.1 %all-reduce.4 = bf16[32,3072]{1,0:T(8,128)(2,1)S(1)} all-reduce(f32[32,3072]{1,0:T(8,128)S(1)} %fusion.5), channel_id=1, replica_groups=mesh['seq'=16,'exp'=32] {'seq'}, use_global_device_ids=true, to_apply=%region_7.0 | all-reduce | flops 98304 | bytes 589824 | tf_op jit(solution)/shard_map/psum | solution.py:30
  266.8 0.7 reduce.1
  267.6 0.1 reshape.12
  267.7 25.8 %all_to_all.25 = bf16[32,2,1536]{2,1,0:T(2,128)(2,1)S(1)} all-to-all(bf16[32,2,1536]{2,1,0:T(2,128)(2,1)S(1)} %reshape.12), channel_id=1, replica_groups=mesh['seq'=16,'exp'=32] {'exp'}, dimensions={0} | all-to-all | bytes 393216 | tf_op jit(solution)/shard_map/all_to_all | solution.py:31
  293.5 0.1 reshape.13
  293.6 1.6 fusion
Async XLA Ops:
  6.5 29.3 %copy-start = (bf16[1,224,3072]{2,1,0:T(8,128)(2,1)S(1)}, bf16[1,224,3072]{2,1,0:T(8,128)(2,1)}, u32[]{:S(2)}) copy-start(bf16[1,224,3072]{2,1,0:T(8,128)(2,1)} %param.4) | copy-start | bytes 4128772
  6.5 185.2 %all-reduce.3.cloned.1.call-start = ((), (), s32[]{:S(2)}) async-start(), calls=%async_computation.2 | async-start | bytes 786432 | tf_op jit(solution)/shard_map/psum | solution.py:24
  64.2 155.2 %copy-start.1 = (bf16[1,192,3072]{2,1,0:T(8,128)(2,1)S(1)}, bf16[1,192,3072]{2,1,0:T(8,128)(2,1)}, u32[]{:S(2)}) copy-start(bf16[1,192,3072]{2,1,0:T(8,128)(2,1)} %param.7) | copy-start | bytes 3538948
Sparse Core Ops, SparseCore 0:
  64.3 127.3 all-reduce.2
where the time goes:
time: 302 us
  blocking collectives  172 us (57%)
  waiting for transfers between devices  107 us (35%)
  between operations  13.4 us (4%)
  matrix products  5.66 us (2%)
    psum x1, waiting for transfers between devices, shards(): total, denom = lax.psum((partial_value, part_sum), 'seq')  107 us
    psum x1, blocking collectives, shards(): out_whole = lax.psum(out_term, 'seq').astype(jnp.bfloat16)  45.1 us
    all_gather x1, blocking collectives, shards(): slot_table = lax.all_gather(slot_keys, 'exp', axis=0, tiled=True)  29.3 us
    pmax x1, blocking collectives, shards(): column_max = lax.pmax(local_max, 'seq')  26.5 us
    all_to_all x1, blocking collectives, shards(): lax.all_to_all(out_whole, 'exp', split_axis=0, concat_axis=0, tiled=True)  25.8 us
    all_to_all x1, blocking collectives, shards(): lax.all_to_all(slot_in, 'exp', split_axis=0, concat_axis=0, tiled=True)  25.1 us
    psum x1, blocking collectives, shards(): total, denom = lax.psum((partial_value, part_sum), 'seq')  20.5 us
  transfers between devices with their start and end apart: 1, of which 1 were waited for; matrix products, arithmetic and copies ran while one was open for 0% of the time, Pallas kernels for 0%

commit v1 on v0

v1 whole, which is shorter than its diff:
```python
import functools

import jax
import jax.numpy as jnp
from jax import lax
from jax.experimental import pallas as pl
from jax.experimental.pallas import tpu as pltpu
from jax.sharding import PartitionSpec as P

F32 = jnp.float32
BF16 = jnp.bfloat16
SEQ = 16
EXP = 32
LANES = 128
D = 3072
BLOCKS = D // LANES
HALF = LANES // 2
FULL = 32
PACKED = 48
STATS = 56
SMALL = 16

VMEM = pl.BlockSpec(memory_space=pltpu.VMEM)


def call(kernel, outs, scratch=(), n_in=1, flops=0, n_bytes=0):
    return pl.pallas_call(
        kernel,
        out_shape=outs,
        in_specs=[VMEM] * n_in,
        out_specs=jax.tree.map(lambda _: VMEM, outs),
        scratch_shapes=list(scratch),
        cost_estimate=pl.CostEstimate(flops=flops, bytes_accessed=n_bytes, transcendentals=0),
        compiler_params=pltpu.CompilerParams(vmem_limit_bytes=24 * 1024 * 1024),
    )


def left_lanes(rows):
    return lax.broadcasted_iota(jnp.int32, (rows, LANES), 1) < HALF


def swap(x):
    return pltpu.roll(x, HALF, 1)


def pack_halves(block):
    top, low = block[:16], block[16:]
    left = left_lanes(16)
    return jnp.where(left, top, swap(low)), jnp.where(left, swap(top), low)


def unpack_halves(even, odd):
    left = left_lanes(16)
    top = jnp.where(left, even, swap(odd))
    low = jnp.where(left, swap(even), odd)
    return jnp.concatenate([top, low], axis=0)


def store_shares(out_ref, term, base):
    for k in range(term.shape[1] // LANES):
        block = base // LANES + k
        piece = term[:, k * LANES : (k + 1) * LANES]
        if block < SEQ:
            out_ref[block, 0:FULL, :] = piece.astype(BF16)
        else:
            even, odd = pack_halves(piece)
            share = 2 * (block - SEQ)
            out_ref[share, FULL:PACKED, :] = even.astype(BF16)
            out_ref[share + 1, FULL:PACKED, :] = odd.astype(BF16)


def load_shares(in_ref, rows_ref):
    for block in range(SEQ):
        rows_ref[:, block * LANES : (block + 1) * LANES] = in_ref[block, 0:FULL, :]
    for j in range(BLOCKS - SEQ):
        even = in_ref[2 * j, FULL:PACKED, :].astype(F32)
        odd = in_ref[2 * j + 1, FULL:PACKED, :].astype(F32)
        block = SEQ + j
        rows_ref[:, block * LANES : (block + 1) * LANES] = unpack_halves(even, odd).astype(BF16)


def dispatch_kernel(patch_ref, keys_ref, out_ref, logits_ref, spread_ref, table_ref):
    spread_ref[...] = keys_ref[...].astype(F32).reshape(EXP * BLOCKS, LANES)
    for k in range(BLOCKS):
        rows = spread_ref[pl.ds(k, EXP, stride=BLOCKS), :]
        table_ref[:, k * LANES : (k + 1) * LANES] = rows.astype(BF16)
    logits = lax.dot_general(
        table_ref[...], patch_ref[...], (((1,), (1,)), ((), ())), preferred_element_type=F32
    )
    logits_ref[...] = logits
    shift = jnp.max(logits, axis=1, keepdims=True).astype(BF16).astype(F32)
    raised = jnp.exp(logits - shift)
    denom = jnp.sum(raised, axis=1, keepdims=True)
    weights = raised.astype(BF16)
    high = denom.astype(BF16).astype(F32)
    low = denom - high
    row = lax.broadcasted_iota(jnp.int32, (EXP, LANES), 0)
    lane = lax.broadcasted_iota(jnp.int32, (EXP, LANES), 1)
    spots = jnp.where(lane == row, shift, 0.0)
    spots += jnp.where(lane == row + EXP, high, 0.0)
    spots += jnp.where(lane == row + 2 * EXP, low, 0.0)
    stats = jnp.broadcast_to(jnp.sum(spots, axis=0, keepdims=True), (STATS - PACKED, LANES)).astype(BF16)
    for share in range(SEQ):
        out_ref[share, PACKED:STATS, :] = stats
    step = 512
    for base in range(0, D, step):
        term = jnp.dot(weights, patch_ref[:, base : base + step], preferred_element_type=F32)
        store_shares(out_ref, term, base)


def store_small(out_ref, full, half):
    half = jnp.concatenate([half, swap(half)], axis=0)
    row = lax.broadcasted_iota(jnp.int32, (SMALL, LANES), 0)
    for e in range(EXP):
        whole = jnp.broadcast_to(full[e : e + 1], (SMALL, LANES))
        part = jnp.broadcast_to(half[e : e + 1], (SMALL, LANES))
        out_ref[e] = jnp.where(row == 0, whole, part).astype(BF16)


def merge_kernel(in_ref, out_ref):
    stats = jnp.concatenate([in_ref[s, PACKED:STATS, :].astype(F32)[0:1] for s in range(SEQ)], axis=0)
    shift = stats
    high = pltpu.roll(stats, LANES - EXP, 1)
    low = pltpu.roll(stats, LANES - 2 * EXP, 1)
    lane = lax.broadcasted_iota(jnp.int32, (SEQ, LANES), 1)
    scale = jnp.exp(shift - jnp.max(shift, axis=0, keepdims=True))
    denom = jnp.sum(scale * (high + low), axis=0, keepdims=True)
    scale = jnp.where(lane < EXP, scale / denom, 0.0)
    scale = jnp.concatenate([scale, jnp.zeros((LANES - SEQ, LANES), F32)], axis=0)
    columns = scale.T
    full = jnp.zeros((FULL, LANES), F32)
    half = jnp.zeros((16, LANES), F32)
    left = left_lanes(16)
    for s in range(SEQ):
        factor = columns[0:EXP, s : s + 1]
        full += factor * in_ref[s, 0:FULL, :].astype(F32)
        packed = jnp.where(left, factor[:16], factor[16:])
        half += packed * in_ref[s, FULL:PACKED, :].astype(F32)
    store_small(out_ref, full, half)


def add_kernel(in_ref, out_ref):
    full = jnp.zeros((FULL, LANES), F32)
    half = jnp.zeros((16, LANES), F32)
    for s in range(SEQ):
        full += in_ref[s, 0:FULL, :].astype(F32)
        half += in_ref[s, FULL:PACKED, :].astype(F32)
    store_small(out_ref, full, half)


def gather_kernel(in_ref, out_ref, spread_ref):
    spread_ref[...] = in_ref[...].astype(F32).reshape(EXP * SMALL, LANES)
    full = spread_ref[pl.ds(0, EXP, stride=SMALL), :].astype(BF16)
    half = spread_ref[pl.ds(1, EXP, stride=SMALL), :]
    half = jnp.where(left_lanes(16), half[:16], swap(half[16:])).astype(BF16)
    for s in range(SEQ):
        out_ref[s, 0:FULL, :] = full
        out_ref[s, FULL:PACKED, :] = half


def ffn_kernel(in_ref, first_ref, second_ref, out_ref, rows_ref):
    load_shares(in_ref, rows_ref)
    hidden = jnp.dot(rows_ref[...], first_ref[...], preferred_element_type=F32)
    activated = jax.nn.gelu(hidden).astype(BF16)
    step = 512
    for base in range(0, D, step):
        term = jnp.dot(activated, second_ref[:, base : base + step], preferred_element_type=F32)
        store_shares(out_ref, term, base)


def mix_kernel(in_ref, logits_ref, out_ref, rows_ref, combine_ref, *, step):
    @pl.when(pl.program_id(0) == 0)
    def _():
        load_shares(in_ref, rows_ref)
        logits = logits_ref[...]
        raised = jnp.exp(logits - jnp.max(logits, axis=0, keepdims=True))
        combine = raised / jnp.sum(raised, axis=0, keepdims=True)
        combine_ref[...] = combine.T.astype(BF16)

    base = pl.multiple_of(pl.program_id(0) * step, step)
    out_ref[...] = jnp.dot(
        combine_ref[...], rows_ref[:, pl.ds(base, step)], preferred_element_type=F32
    ).astype(BF16)


def exchange(x, axis):
    return lax.all_to_all(x, axis, split_axis=0, concat_axis=0, tiled=True)


def shards(patches, slot_keys, w_in, w_out):
    patch_rows = patches[0]
    rows = patch_rows.shape[0]
    sds = jax.ShapeDtypeStruct
    own_key = jnp.broadcast_to(slot_keys.reshape(1, BLOCKS, LANES), (EXP, BLOCKS, LANES))
    keys = exchange(own_key, "exp")
    terms, logits = call(
        dispatch_kernel,
        (sds((SEQ, STATS, LANES), BF16), sds((EXP, rows), F32)),
        [pltpu.VMEM((EXP * BLOCKS, LANES), F32), pltpu.VMEM((EXP, D), BF16)],
        n_in=2,
    )(patch_rows, keys)
    small = sds((EXP, SMALL, LANES), BF16)
    shares = sds((SEQ, PACKED, LANES), BF16)
    spread = [pltpu.VMEM((EXP * SMALL, LANES), F32)]
    slot_part = call(merge_kernel, small)(exchange(terms, "seq"))
    slot_shares = call(gather_kernel, shares, spread)(exchange(slot_part, "exp"))
    out_terms = call(ffn_kernel, shares, [pltpu.VMEM((EXP, D), BF16)], n_in=3)(
        exchange(slot_shares, "seq"), w_in[0], w_out[0]
    )
    out_part = call(add_kernel, small)(exchange(out_terms, "seq"))
    out_shares = call(gather_kernel, shares, spread)(exchange(out_part, "exp"))
    step = 768
    mixed = pl.pallas_call(
        functools.partial(mix_kernel, step=step),
        grid=(D // step,),
        out_shape=sds((rows, D), BF16),
        in_specs=[VMEM, VMEM],
        out_specs=pl.BlockSpec((rows, step), lambda j: (0, j)),
        scratch_shapes=[pltpu.VMEM((EXP, D), BF16), pltpu.VMEM((rows, EXP), BF16)],
        compiler_params=pltpu.CompilerParams(vmem_limit_bytes=24 * 1024 * 1024),
    )(exchange(out_shares, "seq"), logits)
    return mixed[None]


def solution(mesh):
    placed = (P("exp", "seq", None), P("exp", None), P("exp", None, "seq"), P("exp", "seq", None))
    return jax.shard_map(
        shards, mesh=mesh, in_specs=placed, out_specs=P("exp", "seq", None), check_vma=False
    )
```

time: 302 us -> 143 us (0.47)
  the two profiles are of different devices: /device:TPU:1 before, /device:TPU:32 now
where the time goes in v1:
time: 143 us
  blocking collectives  113 us (79%)
  waiting for transfers between devices  14.4 us (10%)
  Pallas kernels  5.92 us (4%)
  starting transfers between devices  5.72 us (4%)
  local copies, waits for them, and re-layouts  3.11 us (2%)
    all_to_all x6, blocking collectives, exchange(): return lax.all_to_all(x, axis, split_axis=0, concat_axis=0, tiled=True)  113 us
    all_to_all x1, waiting for transfers between devices, exchange(): return lax.all_to_all(x, axis, split_axis=0, concat_axis=0, tiled=True)  14.4 us
    all_to_all x1, starting transfers between devices, exchange(): return lax.all_to_all(x, axis, split_axis=0, concat_axis=0, tiled=True)  5.72 us
    unnamed x5, local copies, waits for them, and re-layouts  3.08 us
  transfers between devices with their start and end apart: 1, of which 1 were waited for; matrix products, arithmetic and copies ran while one was open for 1% of the time, Pallas kernels for 0%

profile of v1, /device:TPU:32, one launch (start us, length us, event | category | flops | bytes accessed | tf_op | source)
XLA Modules:
  0.0 142.7 jit_solution(3100691446678886327)
XLA Ops:
  0.0 0.7 reduce
  0.8 15.5 %all_to_all.35.keys_ref = bf16[32,24,128]{2,1,0:T(8,128)(2,1)S(1)} all-to-all(bf16[32,24,128]{2,1,0:T(8,128)(2,1)S(1)} %broadcast_in_dim.11), channel_id=1, replica_groups=mesh['seq'=16,'exp'=32] {'exp'}, dimensions={0} | all-to-all | bytes 393216 | tf_op jit(solution)/shard_map/all_to_all | solution.py:187
  16.3 0.0 copy-start
  16.3 1.3 copy-done
  17.6 1.3 shard_map.46
  18.9 32.4 %all_to_all.36.in_ref = bf16[16,56,128]{2,1,0:T(8,128)(2,1)S(1)} all-to-all(bf16[16,56,128]{2,1,0:T(8,128)(2,1)S(1)} %get-tuple-element.7), channel_id=1, replica_groups=mesh['seq'=16,'exp'=32] {'seq'}, dimensions={0} | all-to-all | bytes 458752 | tf_op jit(solution)/shard_map/all_to_all | solution.py:187
  51.4 0.4 shard_map.47
  51.8 11.2 %all_to_all.37.in_ref = bf16[32,16,128]{2,1,0:T(8,128)(2,1)S(1)} all-to-all(bf16[32,16,128]{2,1,0:T(8,128)(2,1)S(1)} %shard_map.47), channel_id=1, replica_groups=mesh['seq'=16,'exp'=32] {'exp'}, dimensions={0} | all-to-all | bytes 262144 | tf_op jit(solution)/shard_map/all_to_all | solution.py:187
  62.9 0.8 shard_map.48
  63.7 5.7 %all-to-all-start.3 = ((bf16[16,48,128]{2,1,0:T(8,128)(2,1)}), bf16[16,48,128]{2,1,0:T(8,128)(2,1)S(1)}, u32[]{:S(2)}, u32[]{:S(2)}) async-start(bf16[16,48,128]{2,1,0:T(8,128)(2,1)} %shard_map.48), calls=%async_computation.3 | async-start | bytes 393216 | tf_op jit(solution)/shard_map/all_to_all | solution.py:187
  69.4 0.0 copy-start.1
  69.4 1.7 %copy.5 = bf16[1,3072,192]{2,1,0:T(8,128)(2,1)S(1)} copy(bf16[1,3072,192]{1,2,0:T(8,128)(2,1)} %param.6) | data formatting | bytes 2359296 | tf_op args[2]
  71.1 14.4 %all-to-all-done.3.in_ref = bf16[16,48,128]{2,1,0:T(8,128)(2,1)S(1)} async-done(((bf16[16,48,128]{2,1,0:T(8,128)(2,1)}), bf16[16,48,128]{2,1,0:T(8,128)(2,1)S(1)}, u32[]{:S(2)}, u32[]{:S(2)}) %all-to-all-start.3) | async-done | bytes 196640 | tf_op jit(solution)/shard_map/all_to_all | solution.py:187
  85.6 0.0 copy-done.1
  85.6 1.0 shard_map.49
  86.6 21.1 %all_to_all.38.in_ref = bf16[16,48,128]{2,1,0:T(8,128)(2,1)S(1)} all-to-all(bf16[16,48,128]{2,1,0:T(8,128)(2,1)S(1)} %shard_map.49), channel_id=1, replica_groups=mesh['seq'=16,'exp'=32] {'seq'}, dimensions={0} | all-to-all | bytes 393216 | tf_op jit(solution)/shard_map/all_to_all | solution.py:187
  107.6 0.1 shard_map.50
  107.7 11.1 %all_to_all.39.in_ref = bf16[32,16,128]{2,1,0:T(8,128)(2,1)S(1)} all-to-all(bf16[32,16,128]{2,1,0:T(8,128)(2,1)S(1)} %shard_map.50), channel_id=1, replica_groups=mesh['seq'=16,'exp'=32] {'exp'}, dimensions={0} | all-to-all | bytes 262144 | tf_op jit(solution)/shard_map/all_to_all | solution.py:187
  118.9 0.1 shard_map.51
  119.0 21.5 %all_to_all.40.in_ref = bf16[16,48,128]{2,1,0:T(8,128)(2,1)S(1)} all-to-all(bf16[16,48,128]{2,1,0:T(8,128)(2,1)S(1)} %shard_map.51), channel_id=1, replica_groups=mesh['seq'=16,'exp'=32] {'seq'}, dimensions={0} | all-to-all | bytes 393216 | tf_op jit(solution)/shard_map/all_to_all | solution.py:187
  140.5 2.3 %shard_map.52 = bf16[224,3072]{1,0:T(8,128)(2,1)} custom-call(bf16[16,48,128]{2,1,0:T(8,128)(2,1)S(1)} %all_to_all.40.in_ref, f32[32,224]{1,0:T(8,128)S(1)} %get-tuple-element.8.logits_ref), custom_call_target="tpu_custom_call" | custom-call | tf_op jit(solution)/shard_map/pallas_call | solution.py:213
  (1 shorter events, 0.0 us)
Async XLA Ops:
  16.3 1.3 copy-start
  63.7 21.9 %all-to-all-start.3 = ((bf16[16,48,128]{2,1,0:T(8,128)(2,1)}), bf16[16,48,128]{2,1,0:T(8,128)(2,1)S(1)}, u32[]{:S(2)}, u32[]{:S(2)}) async-start(bf16[16,48,128]{2,1,0:T(8,128)(2,1)} %shard_map.48), calls=%async_computation.3 | async-start | bytes 393216 | tf_op jit(solution)/shard_map/all_to_all | solution.py:187
  69.4 16.2 %copy-start.1 = (bf16[1,192,3072]{2,1,0:T(8,128)(2,1)S(1)}, bf16[1,192,3072]{2,1,0:T(8,128)(2,1)}, u32[]{:S(2)}) copy-start(bf16[1,192,3072]{2,1,0:T(8,128)(2,1)} %param.7) | copy-start | bytes 3538948

commit v2 on v0

v2 whole, which is shorter than its diff:
```python
import jax
import jax.numpy as jnp
from jax import lax
from jax.experimental import pallas as pl
from jax.experimental.pallas import tpu as pltpu
from jax.sharding import Mesh, PartitionSpec as P

F32 = jnp.float32
BF16 = jnp.bfloat16
SEQ = 16
EXP = 32
SIDE = 4
PEERS = SEQ * SIDE
LANES = 128
D = 3072
BLOCKS = D // LANES
HALF = LANES // 2
ROWS = 16
VMEM = pl.BlockSpec(memory_space=pltpu.VMEM)
HBM = pl.BlockSpec(memory_space=pltpu.HBM)
SMEM = pl.BlockSpec(memory_space=pltpu.SMEM)
LIMIT = 24 * 1024 * 1024
sds = jax.ShapeDtypeStruct


def call(kernel, outs, in_specs, scratch=(), out_specs=None, flops=0, n_bytes=0):
    return pl.pallas_call(
        kernel,
        out_shape=outs,
        in_specs=in_specs,
        out_specs=jax.tree.map(lambda _: VMEM, outs) if out_specs is None else out_specs,
        scratch_shapes=list(scratch),
        cost_estimate=pl.CostEstimate(flops=flops, bytes_accessed=n_bytes, transcendentals=0),
        compiler_params=pltpu.CompilerParams(vmem_limit_bytes=LIMIT),
    )


def lanes_left():
    return lax.broadcasted_iota(jnp.int32, (8, LANES), 1) < HALF


def rows_top():
    return lax.broadcasted_iota(jnp.int32, (8, LANES), 0) < 4


def swap(x):
    return pltpu.roll(x, HALF, 1)


def turn(x):
    return pltpu.roll(x, 4, 0)


def store_shares(out_ref, term_ref, stats):
    left, top = lanes_left(), rows_top()

    def pair(j, _):
        low = pl.multiple_of(2 * j * LANES, 2 * LANES)
        high = pl.multiple_of((SEQ + j) * LANES, LANES)
        for g in range(SIDE):
            rows = slice(8 * g, 8 * g + 8)
            whole = term_ref[rows, pl.ds(low, 2 * LANES)]
            part = term_ref[rows, pl.ds(high, LANES)]
            other = turn(part)
            even = jnp.where(left, part, swap(other))
            odd = jnp.where(left, swap(part), other)
            if stats is not None:
                even = jnp.where(top, even, stats[g])
                odd = jnp.where(top, odd, stats[g])
            first = jnp.concatenate([whole[:, :LANES], even], axis=0)
            second = jnp.concatenate([whole[:, LANES:], odd], axis=0)
            out_ref[2 * SIDE * j + g] = first.astype(BF16)
            out_ref[2 * SIDE * j + SIDE + g] = second.astype(BF16)
        return 0

    lax.fori_loop(0, SEQ // 2, pair, 0)


def load_shares(in_ref, rows_ref):
    left, top = lanes_left(), rows_top()

    def pair(j, _):
        firsts, seconds, parts = [], [], []
        for g in range(SIDE):
            first = in_ref[2 * SIDE * j + g].astype(F32)
            second = in_ref[2 * SIDE * j + SIDE + g].astype(F32)
            firsts.append(first[:8])
            seconds.append(second[:8])
            even, odd = first[8:], second[8:]
            upper = jnp.where(left, even, swap(odd))
            lower = jnp.where(left, swap(even), odd)
            parts.append(jnp.where(top, upper, turn(lower)))
        low = pl.multiple_of(2 * j * LANES, 2 * LANES)
        high = pl.multiple_of((SEQ + j) * LANES, LANES)
        rows_ref[:, pl.ds(low, LANES)] = jnp.concatenate(firsts, axis=0).astype(BF16)
        rows_ref[:, pl.ds(low + LANES, LANES)] = jnp.concatenate(seconds, axis=0).astype(BF16)
        rows_ref[:, pl.ds(high, LANES)] = jnp.concatenate(parts, axis=0).astype(BF16)
        return 0

    lax.fori_loop(0, SEQ // 2, pair, 0)


def load_kernel(src_ref, out_ref, sem):
    copy = pltpu.make_async_copy(src_ref, out_ref, sem)
    copy.start()
    copy.wait()


def dispatch_kernel(place_ref, patch_ref, keys_ref, out_ref, logits_ref, spread_ref, table_ref, term_ref):
    spread_ref[...] = keys_ref[...].astype(F32).reshape(EXP * BLOCKS, LANES)
    for k in range(BLOCKS):
        rows = spread_ref[pl.ds(k, EXP, stride=BLOCKS), :]
        table_ref[:, k * LANES : (k + 1) * LANES] = rows.astype(BF16)
    logits = lax.dot_general(
        table_ref[...], patch_ref[...], (((1,), (1,)), ((), ())), preferred_element_type=F32
    )
    logits_ref[...] = logits
    shift = jnp.max(logits, axis=1, keepdims=True).astype(BF16).astype(F32)
    raised = jnp.exp(logits - shift)
    denom = jnp.sum(raised, axis=1, keepdims=True)
    weights = raised.astype(BF16)
    high = denom.astype(BF16).astype(F32)
    low = denom - high
    place = place_ref[0]
    lane = lax.broadcasted_iota(jnp.int32, (EXP, LANES), 1)
    spots = jnp.where(lane == place, shift, 0.0)
    spots += jnp.where(lane == place + SEQ, high, 0.0)
    spots += jnp.where(lane == place + 2 * SEQ, low, 0.0)
    stats = []
    for g in range(SIDE):
        tile = spots[8 * g : 8 * g + 8]
        stats.append(turn(tile) + swap(tile))
    for base in range(0, D, 768):
        term_ref[:, base : base + 768] = jnp.dot(
            weights, patch_ref[:, base : base + 768], preferred_element_type=F32
        )
    store_shares(out_ref, term_ref, stats)


def store_cores(out_ref, wholes, halves):
    top = rows_top()
    spread = [jnp.where(top, h, turn(swap(h))) for h in halves]
    low, high = [], []
    for tiles in (wholes, spread):
        for a, b in ((0, 1), (2, 3)):
            low.append(jnp.where(top, tiles[a], turn(tiles[b])))
            high.append(jnp.where(top, turn(tiles[a]), tiles[b]))
    out_ref[0] = jnp.concatenate(low, axis=0).astype(BF16)
    out_ref[1] = jnp.concatenate(high, axis=0).astype(BF16)


def merge_kernel(in_ref, out_ref):
    left, top = lanes_left(), rows_top()
    gathered = []
    for g in range(SIDE):
        total = in_ref[g, :, :].astype(F32)[8:]
        for s in range(1, SEQ):
            total += in_ref[SIDE * s + g, :, :].astype(F32)[8:]
        gathered.append(jnp.where(top, turn(total), swap(total)))
    stats = jnp.concatenate(gathered, axis=0)
    valid = lax.broadcasted_iota(jnp.int32, (EXP, LANES), 1) < SEQ
    largest = jnp.max(jnp.where(valid, stats, -jnp.inf), axis=1, keepdims=True)
    scale = jnp.exp(jnp.where(valid, stats - largest, 0.0))
    denoms = pltpu.roll(stats, LANES - SEQ, 1) + pltpu.roll(stats, LANES - 2 * SEQ, 1)
    denom = jnp.sum(jnp.where(valid, scale * denoms, 0.0), axis=1, keepdims=True)
    scale = scale / denom
    wholes, halves = [], []
    for g in range(SIDE):
        whole = jnp.zeros((8, LANES), F32)
        half = jnp.zeros((8, LANES), F32)
        for s in range(SEQ):
            factor = jnp.broadcast_to(scale[8 * g : 8 * g + 8, s : s + 1], (8, LANES))
            block = in_ref[SIDE * s + g].astype(F32)
            whole += factor * block[:8]
            half += jnp.where(left, factor, turn(factor)) * block[8:]
        wholes.append(whole)
        halves.append(half)
    store_cores(out_ref, wholes, halves)


def add_kernel(in_ref, out_ref):
    wholes, halves = [], []
    for g in range(SIDE):
        total = in_ref[g].astype(F32)
        for s in range(1, SEQ):
            total += in_ref[SIDE * s + g].astype(F32)
        wholes.append(total[:8])
        halves.append(total[8:])
    store_cores(out_ref, wholes, halves)


def regroup_kernel(in_ref, out_ref, spread_ref):
    left = lanes_left()
    for c in range(2):
        both = in_ref[c].astype(F32)
        spread_ref[16 * c : 16 * c + 16, :] = both[:16]
        spread_ref[32 + 16 * c : 48 + 16 * c, :] = both[16:]
    for g in range(SIDE):
        whole = spread_ref[pl.ds(g, 8, stride=SIDE), :]
        half = spread_ref[pl.ds(32 + g, 8, stride=SIDE), :]
        half = jnp.where(left, half, swap(turn(half)))
        block = jnp.concatenate([whole, half], axis=0).astype(BF16)
        for s in range(SEQ):
            out_ref[SIDE * s + g] = block


def ffn_kernel(in_ref, first_ref, second_ref, out_ref, rows_ref, term_ref):
    load_shares(in_ref, rows_ref)
    hidden = lax.dot_general(
        rows_ref[...], first_ref[...], (((1,), (1,)), ((), ())), preferred_element_type=F32
    )
    activated = jax.nn.gelu(hidden).astype(BF16)
    for base in range(0, D, 768):
        term_ref[:, base : base + 768] = jnp.dot(
            activated, second_ref[:, base : base + 768], preferred_element_type=F32
        )
    store_shares(out_ref, term_ref, None)


def combine_kernel(logits_ref, out_ref):
    logits = logits_ref[...]
    raised = jnp.exp(logits - jnp.max(logits, axis=0, keepdims=True))
    combine = raised / jnp.sum(raised, axis=0, keepdims=True)
    out_ref[...] = combine.T.astype(BF16)


def mix_kernel(in_ref, combine_ref, out_ref, rows_ref, mixed_ref, sems):
    load_shares(in_ref, rows_ref)
    copies = []
    step = D // len(MIX_STEPS)
    for j in MIX_STEPS:
        cols = slice(j * step, (j + 1) * step)
        mixed_ref[:, cols] = jnp.dot(
            combine_ref[...], rows_ref[:, cols], preferred_element_type=F32
        ).astype(BF16)
        copies.append(pltpu.make_async_copy(mixed_ref.at[:, cols], out_ref.at[:, cols], sems.at[j]))
        copies[-1].start()
    for copy in copies:
        copy.wait()


MIX_STEPS = range(6)


def exchange(x, axes):
    return lax.all_to_all(x, axes, split_axis=0, concat_axis=0, tiled=True)


def shards(patches, slot_keys, w_in, w_out):
    rows = patches.shape[1]
    wide = sds((PEERS, ROWS, LANES), BF16)
    small = sds((2, 2 * ROWS, LANES), BF16)
    table = pltpu.VMEM((EXP, D), BF16)
    term = pltpu.VMEM((EXP, D), F32)

    own_key = jnp.broadcast_to(slot_keys.reshape(1, BLOCKS, LANES), (EXP, BLOCKS, LANES))
    keys = exchange(own_key, ("x", "core", "y"))
    patch_rows = call(
        load_kernel, sds((rows, D), BF16), [HBM], [pltpu.SemaphoreType.DMA], n_bytes=4 * rows * D
    )(patches[0])
    place = lax.axis_index("seq").astype(jnp.int32).reshape(1)
    terms, logits = call(
        dispatch_kernel,
        (wide, sds((EXP, rows), F32)),
        [SMEM, VMEM, VMEM],
        [pltpu.VMEM((EXP * BLOCKS, LANES), F32), table, term],
    )(place, patch_rows, keys)
    combine = call(combine_kernel, sds((rows, EXP), BF16), [VMEM], n_bytes=1 << 20)(logits)

    spread = [pltpu.VMEM((64, LANES), F32)]
    slot_part = call(merge_kernel, small, [VMEM])(exchange(terms, ("seq", "x")))
    slot_tiles = call(regroup_kernel, wide, [VMEM], spread)(exchange(slot_part, "core"))
    out_terms = call(ffn_kernel, wide, [VMEM] * 3, [table, term])(
        exchange(slot_tiles, ("seq", "y")), w_in[0].T, w_out[0]
    )
    out_part = call(add_kernel, small, [VMEM])(exchange(out_terms, ("seq", "y")))
    out_tiles = call(regroup_kernel, wide, [VMEM], spread)(exchange(out_part, "core"))
    mixed = call(
        mix_kernel,
        sds((rows, D), BF16),
        [VMEM, VMEM],
        [table, pltpu.VMEM((rows, D), BF16), pltpu.SemaphoreType.DMA((len(MIX_STEPS),))],
        out_specs=HBM,
    )(exchange(out_tiles, ("seq", "x")), combine)
    return mixed[None]


def solution(mesh):
    split = Mesh(mesh.devices.reshape(SEQ, SIDE, SIDE, 2), ("seq", "x", "y", "core"))
    exp = ("x", "y", "core")
    placed = (P(exp, "seq", None), P(exp, None), P(exp, None, "seq"), P(exp, "seq", None))
    return jax.shard_map(
        shards, mesh=split, in_specs=placed, out_specs=P(exp, "seq", None), check_vma=False
    )
```

time: 302 us -> 153 us (0.51)
  waiting for transfers between devices: 107 us -> 26.8 us
  blocking collectives: 172 us -> 98.9 us
  starting transfers between devices: 0.01 us -> 15.8 us
  between operations: 13.4 us -> 0.06 us
  Pallas kernels: 0 us -> 7.87 us
  matrix products: 5.66 us -> 0 us
    psum x1 -> x0, waiting for transfers between devices: 107 us -> none  [shards(): total, denom = lax.psum((partial_value, part_sum), 'seq')]
    psum x2 -> x0, blocking collectives: 65.7 us -> none  [the longest x1 45.1 us: shards(): out_whole = lax.psum(out_term, 'seq').astype(jnp.bfloat16)]
    all_to_all x2 -> x5, blocking collectives: 50.8 us -> 98.9 us  [exchange(): return lax.all_to_all(x, axes, split_axis=0, concat_axis=0, tiled=True)]
    all_gather x1 -> x0, blocking collectives: 29.3 us -> none  [shards(): slot_table = lax.all_gather(slot_keys, 'exp', axis=0, tiled=True)]
    all_to_all x0 -> x2, waiting for transfers between devices: none -> 26.8 us  [exchange(): return lax.all_to_all(x, axes, split_axis=0, concat_axis=0, tiled=True)]
    pmax x1 -> x0, blocking collectives: 26.5 us -> none  [shards(): column_max = lax.pmax(local_max, 'seq')]
    all_to_all x0 -> x2, starting transfers between devices: none -> 15.8 us  [exchange(): return lax.all_to_all(x, axes, split_axis=0, concat_axis=0, tiled=True)]
    pallas_call x0 -> x9, Pallas kernels: none -> 7.87 us  [the longest x1 2.22 us: shards(): call(ffn_kernel, wide, [VMEM] * 3, [table, term])]
  transfers between devices with their start and end apart: 1 -> 2, of which waited for: 1 -> 2; matrix products, arithmetic and copies ran while one was open for 0% -> 0% of each run, Pallas kernels for 0% -> 0%
where the time goes in v2:
time: 153 us; the launch traced here: 152 us
  blocking collectives  98.9 us (65%)
  waiting for transfers between devices  26.8 us (18%)
  starting transfers between devices  15.8 us (10%)
  Pallas kernels  7.87 us (5%)
  local copies, waits for them, and re-layouts  2.05 us (1%)
    all_to_all x5, blocking collectives, exchange(): return lax.all_to_all(x, axes, split_axis=0, concat_axis=0, tiled=True)  98.9 us
    all_to_all x2, waiting for transfers between devices, exchange(): return lax.all_to_all(x, axes, split_axis=0, concat_axis=0, tiled=True)  26.8 us
    all_to_all x2, starting transfers between devices, exchange(): return lax.all_to_all(x, axes, split_axis=0, concat_axis=0, tiled=True)  15.8 us
  transfers between devices with their start and end apart: 2, of which 2 were waited for; matrix products, arithmetic and copies ran while one was open for 0% of the time, Pallas kernels for 0%

profile of v2, /device:TPU:1, one launch (start us, length us, event | category | flops | bytes accessed | tf_op | source)
XLA Modules:
  0.0 152.2 jit_solution(11810660487810764993)
XLA Ops:
  0.0 0.7 reduce
  0.7 0.7 broadcast_in_dim.11
  1.5 10.4 %all-to-all-start = ((bf16[32,24,128]{2,1,0:T(8,128)(2,1)}), bf16[32,24,128]{2,1,0:T(8,128)(2,1)S(1)}, u32[]{:S(2)}, u32[]{:S(2)}) async-start(bf16[32,24,128]{2,1,0:T(8,128)(2,1)} %broadcast_in_dim.11), calls=%async_computation | async-start | bytes 393216 | tf_op jit(solution)/shard_map/all_to_all | solution.py:246
  11.9 0.0 copy-start
  11.9 1.3 copy-done
  13.2 0.2 shard_map.46.patch_ref
  13.4 6.8 %all-to-all-done.keys_ref = bf16[32,24,128]{2,1,0:T(8,128)(2,1)S(1)} async-done(((bf16[32,24,128]{2,1,0:T(8,128)(2,1)}), bf16[32,24,128]{2,1,0:T(8,128)(2,1)S(1)}, u32[]{:S(2)}, u32[]{:S(2)}) %all-to-all-start) | async-done | bytes 196640 | tf_op jit(solution)/shard_map/all_to_all | solution.py:246
  20.2 0.0 copy-start.1
  20.2 0.0 copy-start.2
  20.2 1.9 %shard_map.47 = (bf16[64,16,128]{2,1,0:T(8,128)(2,1)S(1)}, f32[32,224]{1,0:T(8,128)S(1)}) custom-call(s32[1]{0:T(128)} %bitcast.place_ref, bf16[224,3072]{1,0:T(8,128)(2,1)S(1)} %shard_map.46.patch_ref, bf16[32,24,128]{2,1,0:T(8,128)(2,1)S(1)} %all-to-all-done.keys_ref), custom_call_target="tpu_custom_call" | custom-call | tf_op jit(solution)/shard_map/pallas_call | solution.py:262
  22.0 34.2 %all_to_all.35.in_ref = bf16[64,16,128]{2,1,0:T(8,128)(2,1)S(1)} all-to-all(bf16[64,16,128]{2,1,0:T(8,128)(2,1)S(1)} %get-tuple-element.7), channel_id=1, replica_groups=mesh['seq'=16,'x'=4,'y'=4,'core'=2] {'seq','x'}, dimensions={0} | all-to-all | bytes 524288 | tf_op jit(solution)/shard_map/all_to_all | solution.py:246
  56.2 0.5 shard_map.48
  56.7 7.1 %all_to_all.36.in_ref = bf16[2,32,128]{2,1,0:T(8,128)(2,1)S(1)} all-to-all(bf16[2,32,128]{2,1,0:T(8,128)(2,1)S(1)} %shard_map.48), channel_id=1, replica_groups=mesh['seq'=16,'x'=4,'y'=4,'core'=2] {'core'}, dimensions={0} | all-to-all | bytes 32768 | tf_op jit(solution)/shard_map/all_to_all | solution.py:246
  63.8 0.1 shard_map.49
  63.9 24.3 %all_to_all.37.in_ref = bf16[64,16,128]{2,1,0:T(8,128)(2,1)S(1)} all-to-all(bf16[64,16,128]{2,1,0:T(8,128)(2,1)S(1)} %shard_map.49), channel_id=1, replica_groups=mesh['seq'=16,'x'=4,'y'=4,'core'=2] {'seq','y'}, dimensions={0} | all-to-all | bytes 524288 | tf_op jit(solution)/shard_map/all_to_all | solution.py:246
  88.2 0.0 copy-done.1
  88.2 0.0 copy-done.2
  88.2 2.2 %shard_map.50 = bf16[64,16,128]{2,1,0:T(8,128)(2,1)S(1)} custom-call(bf16[64,16,128]{2,1,0:T(8,128)(2,1)S(1)} %all_to_all.37.in_ref, bf16[192,3072]{1,0:T(8,128)(2,1)S(1)} %bitcast.9, bf16[192,3072]{1,0:T(8,128)(2,1)S(1)} %bitcast.10), custom_call_target="tpu_custom_call" | custom-call | tf_op jit(solution)/shard_map/pallas_call | solution.py:273
  90.4 25.1 %all_to_all.38.in_ref = bf16[64,16,128]{2,1,0:T(8,128)(2,1)S(1)} all-to-all(bf16[64,16,128]{2,1,0:T(8,128)(2,1)S(1)} %shard_map.50), channel_id=1, replica_groups=mesh['seq'=16,'x'=4,'y'=4,'core'=2] {'seq','y'}, dimensions={0} | all-to-all | bytes 524288 | tf_op jit(solution)/shard_map/all_to_all | solution.py:246
  115.5 0.1 shard_map.51
  115.6 8.3 %all_to_all.39.in_ref = bf16[2,32,128]{2,1,0:T(8,128)(2,1)S(1)} all-to-all(bf16[2,32,128]{2,1,0:T(8,128)(2,1)S(1)} %shard_map.51), channel_id=1, replica_groups=mesh['seq'=16,'x'=4,'y'=4,'core'=2] {'core'}, dimensions={0} | all-to-all | bytes 32768 | tf_op jit(solution)/shard_map/all_to_all | solution.py:246
  123.9 0.8 shard_map.52
  124.7 5.3 %all-to-all-start.6 = ((bf16[64,16,128]{2,1,0:T(8,128)(2,1)}), bf16[64,16,128]{2,1,0:T(8,128)(2,1)S(1)}, u32[]{:S(2)}, u32[]{:S(2)}) async-start(bf16[64,16,128]{2,1,0:T(8,128)(2,1)} %shard_map.52), calls=%async_computation.6 | async-start | bytes 524288 | tf_op jit(solution)/shard_map/all_to_all | solution.py:246
  130.0 0.1 shard_map.53.combine_ref
  130.2 20.1 %all-to-all-done.6.in_ref = bf16[64,16,128]{2,1,0:T(8,128)(2,1)S(1)} async-done(((bf16[64,16,128]{2,1,0:T(8,128)(2,1)}), bf16[64,16,128]{2,1,0:T(8,128)(2,1)S(1)}, u32[]{:S(2)}, u32[]{:S(2)}) %all-to-all-start.6) | async-done | bytes 262176 | tf_op jit(solution)/shard_map/all_to_all | solution.py:246
  150.2 1.9 %shard_map.54 = bf16[224,3072]{1,0:T(8,128)(2,1)} custom-call(bf16[64,16,128]{2,1,0:T(8,128)(2,1)S(1)} %all-to-all-done.6.in_ref, bf16[224,32]{1,0:T(8,128)(2,1)S(1)} %shard_map.53.combine_ref), custom_call_target="tpu_custom_call" | custom-call | tf_op jit(solution)/shard_map/pallas_call | solution.py:278
Async XLA Ops:
  1.5 18.7 %all-to-all-start = ((bf16[32,24,128]{2,1,0:T(8,128)(2,1)}), bf16[32,24,128]{2,1,0:T(8,128)(2,1)S(1)}, u32[]{:S(2)}, u32[]{:S(2)}) async-start(bf16[32,24,128]{2,1,0:T(8,128)(2,1)} %broadcast_in_dim.11), calls=%async_computation | async-start | bytes 393216 | tf_op jit(solution)/shard_map/all_to_all | solution.py:246
  11.9 1.3 copy-start
  20.2 68.0 %copy-start.1 = (bf16[1,3072,192]{1,2,0:T(8,128)(2,1)S(1)}, bf16[1,3072,192]{1,2,0:T(8,128)(2,1)}, u32[]{:S(2)}) copy-start(bf16[1,3072,192]{1,2,0:T(8,128)(2,1)} %param.6) | copy-start | bytes 3538948
  20.2 68.0 %copy-start.2 = (bf16[1,192,3072]{2,1,0:T(8,128)(2,1)S(1)}, bf16[1,192,3072]{2,1,0:T(8,128)(2,1)}, u32[]{:S(2)}) copy-start(bf16[1,192,3072]{2,1,0:T(8,128)(2,1)} %param.7) | copy-start | bytes 3538948
  124.7 25.6 %all-to-all-start.6 = ((bf16[64,16,128]{2,1,0:T(8,128)(2,1)}), bf16[64,16,128]{2,1,0:T(8,128)(2,1)S(1)}, u32[]{:S(2)}, u32[]{:S(2)}) async-start(bf16[64,16,128]{2,1,0:T(8,128)(2,1)} %shard_map.52), calls=%async_computation.6 | async-start | bytes 524288 | tf_op jit(solution)/shard_map/all_to_all | solution.py:246

commit v3 on v0

v3 whole, which is shorter than its diff:
```python
import jax
import jax.numpy as jnp
from jax import lax
from jax.experimental import pallas as pl
from jax.experimental.pallas import tpu as pltpu
from jax.sharding import Mesh, PartitionSpec as P

F32 = jnp.float32
BF16 = jnp.bfloat16
SIDE = 4
CORES = 2
EXP = SIDE * SIDE * CORES
LANES = 128
D = 3072
BLOCKS = D // LANES
SHARE = BLOCKS // SIDE
PAIRS = SHARE // 2
PEERS = SIDE * SIDE
WIDE = 8 * SHARE
NARROW = 16 * SHARE
VMEM = pl.BlockSpec(memory_space=pltpu.VMEM)
SMEM = pl.BlockSpec(memory_space=pltpu.SMEM)
ANY = pl.BlockSpec(memory_space=pl.ANY)
LIMIT = 24 * 1024 * 1024
sds = jax.ShapeDtypeStruct


def call(kernel, outs, in_specs, scratch=(), out_specs=None):
    return pl.pallas_call(
        kernel,
        out_shape=outs,
        in_specs=in_specs,
        out_specs=jax.tree.map(lambda _: VMEM, outs) if out_specs is None else out_specs,
        scratch_shapes=list(scratch),
        compiler_params=pltpu.CompilerParams(vmem_limit_bytes=LIMIT),
    )


def rows_top():
    return lax.broadcasted_iota(jnp.int32, (8, LANES), 0) < 4


def swap(x):
    return pltpu.roll(x, LANES // 2, 1)


def turn(x):
    return pltpu.roll(x, 4, 0)


def store_share(out_ref, z, term):
    for g in range(SIDE):
        tiles = term[8 * g : 8 * g + 8]
        for m in range(PAIRS):
            low = tiles[:, 2 * m * LANES : (2 * m + 1) * LANES]
            high = tiles[:, (2 * m + 1) * LANES : (2 * m + 2) * LANES]
            pair = jnp.concatenate([low, high], axis=0).astype(BF16)
            out_ref[SIDE * z + g, 16 * m : 16 * m + 16, :] = pair


def load_share(in_ref, z):
    columns = []
    for m in range(PAIRS):
        pairs = [in_ref[SIDE * z + g, 16 * m : 16 * m + 16, :].astype(F32) for g in range(SIDE)]
        columns.append(jnp.concatenate([p[:8] for p in pairs], axis=0))
        columns.append(jnp.concatenate([p[8:] for p in pairs], axis=0))
    return jnp.concatenate(columns, axis=1).astype(BF16)


def spread_stats(place, shift, denom):
    lane = lax.broadcasted_iota(jnp.int32, (shift.shape[0], LANES), 1)
    high = denom.astype(BF16).astype(F32)
    stats = jnp.where(lane == place, shift, 0.0)
    stats = jnp.where(lane == place + SIDE, high, stats)
    return jnp.where(lane == place + 2 * SIDE, denom - high, stats)


def merge_stats(stats):
    valid = lax.broadcasted_iota(jnp.int32, stats.shape, 1) < SIDE
    largest = jnp.max(jnp.where(valid, stats, -jnp.inf), axis=1, keepdims=True)
    scale = jnp.exp(jnp.where(valid, stats - largest, 0.0))
    parts = pltpu.roll(stats, LANES - SIDE, 1) + pltpu.roll(stats, LANES - 2 * SIDE, 1)
    denom = jnp.sum(jnp.where(valid, scale * parts, 0.0), axis=1, keepdims=True)
    return largest, scale, denom


def dispatch_kernel(place_ref, patch_ref, keys_ref, out_ref, combine_ref, spread_ref, table_ref):
    spread_ref[...] = keys_ref[...].astype(F32).reshape(EXP * BLOCKS, LANES)
    for k in range(BLOCKS):
        rows = spread_ref[pl.ds(k, EXP, stride=BLOCKS), :]
        table_ref[:, k * LANES : (k + 1) * LANES] = rows.astype(BF16)
    logits = lax.dot_general(
        table_ref[...], patch_ref[0], (((1,), (1,)), ((), ())), preferred_element_type=F32
    )
    shift = jnp.max(logits, axis=1, keepdims=True).astype(BF16).astype(F32)
    raised = jnp.exp(logits - shift)
    denom = jnp.sum(raised, axis=1, keepdims=True)
    weights = raised.astype(BF16)
    stats = spread_stats(place_ref[0], shift, denom).astype(BF16)
    for z in range(SIDE):
        base = z * SHARE * LANES
        columns = patch_ref[0, :, base : base + SHARE * LANES]
        store_share(out_ref, z, jnp.dot(weights, columns, preferred_element_type=F32))
        for g in range(SIDE):
            out_ref[SIDE * z + g, WIDE : WIDE + 8, :] = stats[8 * g : 8 * g + 8]
    raised = jnp.exp(logits - jnp.max(logits, axis=0, keepdims=True))
    combine = raised / jnp.sum(raised, axis=0, keepdims=True)
    combine_ref[...] = combine.T.astype(BF16)


def store_cores(out_ref, row, tiles):
    top = rows_top()
    low = [jnp.where(top, tiles[a], turn(tiles[a + 1])) for a in (0, 2)]
    high = [jnp.where(top, turn(tiles[a]), tiles[a + 1]) for a in (0, 2)]
    out_ref[0, row : row + 16, :] = jnp.concatenate(low, axis=0).astype(BF16)
    out_ref[1, row : row + 16, :] = jnp.concatenate(high, axis=0).astype(BF16)


def copy_cores(out_ref):
    for h in range(1, SIDE):
        for c in range(CORES):
            out_ref[CORES * h + c] = out_ref[c]


def sum_near(in_ref, out_ref, factor):
    for m in range(PAIRS):
        lows, highs = [], []
        for g in range(SIDE):
            low = high = None
            for z in range(SIDE):
                pair = in_ref[SIDE * z + g, 16 * m : 16 * m + 16, :].astype(F32)
                a, b = pair[:8], pair[8:]
                if factor is not None:
                    a, b = factor[g][z] * a, factor[g][z] * b
                low, high = (a, b) if z == 0 else (low + a, high + b)
            lows.append(low)
            highs.append(high)
        store_cores(out_ref, 32 * m, lows)
        store_cores(out_ref, 32 * m + 16, highs)


def merge_near_kernel(place_ref, in_ref, out_ref):
    gathered = []
    for g in range(SIDE):
        total = in_ref[g, WIDE : WIDE + 8, :].astype(F32)
        for z in range(1, SIDE):
            total += in_ref[SIDE * z + g, WIDE : WIDE + 8, :].astype(F32)
        gathered.append(total)
    largest, scale, denom = merge_stats(jnp.concatenate(gathered, axis=0))
    factor = [
        [jnp.broadcast_to(scale[8 * g : 8 * g + 8, z : z + 1], (8, LANES)) for z in range(SIDE)]
        for g in range(SIDE)
    ]
    sum_near(in_ref, out_ref, factor)
    stats = spread_stats(place_ref[0], largest, denom)
    top = rows_top()
    t = [stats[8 * g : 8 * g + 8] for g in range(SIDE)]
    low = jnp.where(top, t[0], turn(t[1])) + swap(jnp.where(top, t[2], turn(t[3])))
    high = jnp.where(top, turn(t[0]), t[1]) + swap(jnp.where(top, turn(t[2]), t[3]))
    out_ref[0, NARROW : NARROW + 8, :] = low.astype(BF16)
    out_ref[1, NARROW : NARROW + 8, :] = high.astype(BF16)
    copy_cores(out_ref)


def add_near_kernel(in_ref, out_ref):
    sum_near(in_ref, out_ref, None)
    copy_cores(out_ref)


def sum_far(in_ref, out_ref, spread_ref, factor):
    for k in range(SHARE):
        for c in range(CORES):
            total = None
            for h in range(SIDE):
                rows = in_ref[CORES * h + c, 16 * k : 16 * k + 16, :].astype(F32)
                if factor is not None:
                    rows = factor[c][h] * rows
                total = rows if h == 0 else total + rows
            spread_ref[32 * k + 16 * c : 32 * k + 16 * c + 16, :] = total
    for g in range(SIDE):
        for m in range(PAIRS):
            low = spread_ref[pl.ds(64 * m + g, 8, stride=SIDE), :]
            high = spread_ref[pl.ds(64 * m + 32 + g, 8, stride=SIDE), :]
            pair = jnp.concatenate([low, high], axis=0).astype(BF16)
            for z in range(SIDE):
                out_ref[SIDE * z + g, 16 * m : 16 * m + 16, :] = pair


def merge_far_kernel(in_ref, out_ref, spread_ref):
    gathered = []
    for c in range(CORES):
        total = in_ref[c, NARROW : NARROW + 8, :].astype(F32)
        for h in range(1, SIDE):
            total += in_ref[CORES * h + c, NARROW : NARROW + 8, :].astype(F32)
        gathered += [total, swap(total)]
    _, scale, denom = merge_stats(jnp.concatenate(gathered, axis=0))
    scale = scale / denom
    factor = [
        [jnp.broadcast_to(scale[16 * c : 16 * c + 16, h : h + 1], (16, LANES)) for h in range(SIDE)]
        for c in range(CORES)
    ]
    sum_far(in_ref, out_ref, spread_ref, factor)


def add_far_kernel(in_ref, out_ref, spread_ref):
    sum_far(in_ref, out_ref, spread_ref, None)


def ffn_kernel(in_ref, first_ref, second_ref, out_ref):
    hidden = None
    for z in range(SIDE):
        base = z * SHARE * LANES
        term = lax.dot_general(
            load_share(in_ref, z),
            first_ref[0, :, base : base + SHARE * LANES],
            (((1,), (1,)), ((), ())),
            preferred_element_type=F32,
        )
        hidden = term if z == 0 else hidden + term
    activated = jax.nn.gelu(hidden).astype(BF16)
    for z in range(SIDE):
        base = z * SHARE * LANES
        columns = second_ref[0, :, base : base + SHARE * LANES]
        store_share(out_ref, z, jnp.dot(activated, columns, preferred_element_type=F32))


def mix_kernel(in_ref, combine_ref, out_ref, mixed_ref, sems):
    copies = []
    for z in range(SIDE):
        columns = slice(z * SHARE * LANES, (z + 1) * SHARE * LANES)
        mixed_ref[:, columns] = jnp.dot(
            combine_ref[...], load_share(in_ref, z), preferred_element_type=F32
        ).astype(BF16)
        copy = pltpu.make_async_copy(mixed_ref.at[:, columns], out_ref.at[0, :, columns], sems.at[z])
        copy.start()
        copies.append(copy)
    for copy in copies:
        copy.wait()


def exchange(x, *axes):
    return lax.all_to_all(x, axes, split_axis=0, concat_axis=0, tiled=True)


def shards(patches, slot_keys, w_in, w_out):
    rows = patches.shape[1]
    wide = sds((PEERS, WIDE, LANES), BF16)
    narrow = sds((SIDE * CORES, NARROW, LANES), BF16)
    wide_stats = sds((PEERS, WIDE + 8, LANES), BF16)
    narrow_stats = sds((SIDE * CORES, NARROW + 8, LANES), BF16)
    place_near = lax.axis_index("zl").astype(jnp.int32).reshape(1)
    place_far = lax.axis_index("zh").astype(jnp.int32).reshape(1)

    own_key = jnp.broadcast_to(slot_keys.reshape(1, BLOCKS, LANES), (EXP, BLOCKS, LANES))
    own_key, place_near, place_far = lax.optimization_barrier((own_key, place_near, place_far))
    keys = exchange(own_key, "x", "core", "y")
    terms, combine = call(
        dispatch_kernel,
        (wide_stats, sds((rows, EXP), BF16)),
        [SMEM, VMEM, VMEM],
        [pltpu.VMEM((EXP * BLOCKS, LANES), F32), pltpu.VMEM((EXP, D), BF16)],
    )(place_near, patches, keys)

    spread = [pltpu.VMEM((32 * SHARE, LANES), F32)]
    near = call(merge_near_kernel, narrow_stats, [SMEM, VMEM])(place_far, exchange(terms, "zl", "x"))
    slot_tiles = call(merge_far_kernel, wide, [VMEM], spread)(exchange(near, "zh", "core"))
    out_terms = call(ffn_kernel, wide, [VMEM] * 3)(
        exchange(slot_tiles, "zl", "y"), jnp.swapaxes(w_in, 1, 2), w_out
    )
    near = call(add_near_kernel, narrow, [VMEM])(exchange(out_terms, "zl", "y"))
    out_tiles = call(add_far_kernel, wide, [VMEM], spread)(exchange(near, "zh", "core"))
    return call(
        mix_kernel,
        sds((1, rows, D), BF16),
        [VMEM, VMEM],
        [pltpu.VMEM((rows, D), BF16), pltpu.SemaphoreType.DMA((SIDE,))],
        out_specs=ANY,
    )(exchange(out_tiles, "zl", "x"), combine)


def solution(mesh):
    split = Mesh(
        mesh.devices.reshape(SIDE, SIDE, SIDE, SIDE, CORES), ("zh", "zl", "x", "y", "core")
    )
    seq, exp = ("zh", "zl"), ("x", "y", "core")
    placed = (P(exp, seq, None), P(exp, None), P(exp, None, seq), P(exp, seq, None))
    return jax.shard_map(
        shards, mesh=split, in_specs=placed, out_specs=P(exp, seq, None), check_vma=False
    )
```

time: 302 us -> 130 us (0.43)
  waiting for transfers between devices: 107 us -> 0 us
  blocking collectives: 172 us -> 123 us
  between operations: 13.4 us -> 0.04 us
  matrix products: 5.66 us -> 0 us
  Pallas kernels: 0 us -> 4.32 us
    psum x1 -> x0, waiting for transfers between devices: 107 us -> none  [shards(): total, denom = lax.psum((partial_value, part_sum), 'seq')]
    all_to_all x2 -> x7, blocking collectives: 50.8 us -> 123 us  [exchange(): return lax.all_to_all(x, axes, split_axis=0, concat_axis=0, tiled=True)]
    psum x2 -> x0, blocking collectives: 65.7 us -> none  [the longest x1 45.1 us: shards(): out_whole = lax.psum(out_term, 'seq').astype(jnp.bfloat16)]
    all_gather x1 -> x0, blocking collectives: 29.3 us -> none  [shards(): slot_table = lax.all_gather(slot_keys, 'exp', axis=0, tiled=True)]
    pmax x1 -> x0, blocking collectives: 26.5 us -> none  [shards(): column_max = lax.pmax(local_max, 'seq')]
    dot_general x4 -> x0, matrix products: 5.66 us -> none  [the longest x1 2.25 us: shards(): jnp.dot(activated, second_proj, preferred_element_type=jnp.float32)]
    pallas_call x0 -> x7, Pallas kernels: none -> 4.32 us  [the longest x1 1.35 us: shards(): call(mix_kernel, sds((1, rows, D), BF16), [VMEM, VMEM], [pltpu.VMEM((rows...]
  transfers between devices with their start and end apart: 1 -> 0, of which waited for: 1 -> 0; matrix products, arithmetic and copies ran while one was open for 0% -> 0% of each run, Pallas kernels for 0% -> 0%
where the time goes in v3:
time: 130 us; the launch traced here: 129 us
  blocking collectives  123 us (95%)
  Pallas kernels  4.32 us (3%)
  local copies, waits for them, and re-layouts  1.38 us (1%)
    all_to_all x7, blocking collectives, exchange(): return lax.all_to_all(x, axes, split_axis=0, concat_axis=0, tiled=True)  123 us

profile of v3, /device:TPU:1, one launch (start us, length us, event | category | flops | bytes accessed | tf_op | source)
XLA Modules:
  0.0 129.3 jit_solution(11538424811118609820)
XLA Ops:
  0.0 0.7 reduce
  0.8 17.8 %all_to_all.35.keys_ref = bf16[32,24,128]{2,1,0:T(8,128)(2,1)S(1)} all-to-all(bf16[32,24,128]{2,1,0:T(8,128)(2,1)S(1)} %broadcast_in_dim.8), channel_id=1, replica_groups=mesh['zh'=4,'zl'=4,'x'=4,'y'=4,'core'=2] {'x','core','y'}, dimensions={0} | all-to-all | bytes 393216 | tf_op jit(solution)/shard_map/all_to_all | solution.py:242
  18.6 0.0 copy-start
  18.6 1.3 %copy-done = bf16[1,224,3072]{2,1,0:T(8,128)(2,1)S(1)} copy-done((bf16[1,224,3072]{2,1,0:T(8,128)(2,1)S(1)}, bf16[1,224,3072]{2,1,0:T(8,128)(2,1)}, u32[]{:S(2)}) %copy-start) | copy-done | bytes 1376280
  19.9 0.0 copy-start.2
  19.9 1.2 shard_map.46
  21.2 0.0 copy-start.1
  21.2 14.5 %all_to_all.36.in_ref = bf16[16,56,128]{2,1,0:T(8,128)(2,1)S(1)} all-to-all(bf16[16,56,128]{2,1,0:T(8,128)(2,1)S(1)} %get-tuple-element.13), channel_id=1, replica_groups=mesh['zh'=4,'zl'=4,'x'=4,'y'=4,'core'=2] {'zl','x'}, dimensions={0} | all-to-all | bytes 458752 | tf_op jit(solution)/shard_map/all_to_all | solution.py:242
  35.6 0.3 shard_map.47
  35.9 28.0 %all_to_all.37.in_ref = bf16[8,104,128]{2,1,0:T(8,128)(2,1)S(1)} all-to-all(bf16[8,104,128]{2,1,0:T(8,128)(2,1)S(1)} %shard_map.47), channel_id=1, replica_groups=mesh['zh'=4,'zl'=4,'x'=4,'y'=4,'core'=2] {'zh','core'}, dimensions={0} | all-to-all | bytes 425984 | tf_op jit(solution)/shard_map/all_to_all | solution.py:242
  63.9 0.4 shard_map.48
  64.3 16.8 %all_to_all.38.in_ref = bf16[16,48,128]{2,1,0:T(8,128)(2,1)S(1)} all-to-all(bf16[16,48,128]{2,1,0:T(8,128)(2,1)S(1)} %shard_map.48), channel_id=1, replica_groups=mesh['zh'=4,'zl'=4,'x'=4,'y'=4,'core'=2] {'zl','y'}, dimensions={0} | all-to-all | bytes 393216 | tf_op jit(solution)/shard_map/all_to_all | solution.py:242
  81.2 0.0 copy-done.2
  81.2 0.0 copy-done.1
  81.2 1.0 shard_map.49
  82.2 12.3 %all_to_all.39.in_ref = bf16[16,48,128]{2,1,0:T(8,128)(2,1)S(1)} all-to-all(bf16[16,48,128]{2,1,0:T(8,128)(2,1)S(1)} %shard_map.49), channel_id=1, replica_groups=mesh['zh'=4,'zl'=4,'x'=4,'y'=4,'core'=2] {'zl','y'}, dimensions={0} | all-to-all | bytes 393216 | tf_op jit(solution)/shard_map/all_to_all | solution.py:242
  94.5 18.2 %all_to_all.40.in_ref = bf16[8,96,128]{2,1,0:T(8,128)(2,1)S(1)} all-to-all(bf16[8,96,128]{2,1,0:T(8,128)(2,1)S(1)} %shard_map.50), channel_id=1, replica_groups=mesh['zh'=4,'zl'=4,'x'=4,'y'=4,'core'=2] {'zh','core'}, dimensions={0} | all-to-all | bytes 393216 | tf_op jit(solution)/shard_map/all_to_all | solution.py:242
  112.8 15.2 %all_to_all.41.in_ref = bf16[16,48,128]{2,1,0:T(8,128)(2,1)S(1)} all-to-all(bf16[16,48,128]{2,1,0:T(8,128)(2,1)S(1)} %shard_map.51), channel_id=1, replica_groups=mesh['zh'=4,'zl'=4,'x'=4,'y'=4,'core'=2] {'zl','x'}, dimensions={0} | all-to-all | bytes 393216 | tf_op jit(solution)/shard_map/all_to_all | solution.py:242
  128.0 1.4 %shard_map.52 = bf16[1,224,3072]{2,1,0:T(8,128)(2,1)} custom-call(bf16[16,48,128]{2,1,0:T(8,128)(2,1)S(1)} %all_to_all.41.in_ref, bf16[224,32]{1,0:T(8,128)(2,1)S(1)} %get-tuple-element.14.combine_ref), custom_call_target="tpu_custom_call" | custom-call | tf_op jit(solution)/shard_map/pallas_call | solution.py:272
  (3 shorter events, 0.1 us)
Async XLA Ops:
  18.6 1.3 %copy-start = (bf16[1,224,3072]{2,1,0:T(8,128)(2,1)S(1)}, bf16[1,224,3072]{2,1,0:T(8,128)(2,1)}, u32[]{:S(2)}) copy-start(bf16[1,224,3072]{2,1,0:T(8,128)(2,1)} %patch_ref.1) | copy-start | bytes 4128772
  19.9 61.2 %copy-start.2 = (bf16[1,192,3072]{2,1,0:T(8,128)(2,1)S(1)}, bf16[1,192,3072]{2,1,0:T(8,128)(2,1)}, u32[]{:S(2)}) copy-start(bf16[1,192,3072]{2,1,0:T(8,128)(2,1)} %second_ref.1) | copy-start | bytes 3538948
  21.2 60.0 %copy-start.1 = (bf16[1,3072,192]{1,2,0:T(8,128)(2,1)S(1)}, bf16[1,3072,192]{1,2,0:T(8,128)(2,1)}, u32[]{:S(2)}) copy-start(bf16[1,3072,192]{1,2,0:T(8,128)(2,1)} %param.6) | copy-start | bytes 3538948

commit v4 on v3

v4 whole, which is shorter than its diff:
```python
import jax
import jax.numpy as jnp
from jax import lax
from jax.experimental import pallas as pl
from jax.experimental.pallas import tpu as pltpu
from jax.sharding import Mesh, PartitionSpec as P

F32 = jnp.float32
BF16 = jnp.bfloat16
SIDE = 4
CORES = 2
EXP = SIDE * SIDE * CORES
LANES = 128
D = 3072
BLOCKS = D // LANES
SHARE = BLOCKS // SIDE
PAIRS = SHARE // 2
PEERS = SIDE * SIDE
TALL = 16 * SHARE
WIDE = 8 * SHARE
VMEM = pl.BlockSpec(memory_space=pltpu.VMEM)
SMEM = pl.BlockSpec(memory_space=pltpu.SMEM)
ANY = pl.BlockSpec(memory_space=pl.ANY)
LIMIT = 24 * 1024 * 1024
sds = jax.ShapeDtypeStruct


def call(kernel, outs, in_specs, scratch=(), out_specs=None):
    return pl.pallas_call(
        kernel,
        out_shape=outs,
        in_specs=in_specs,
        out_specs=jax.tree.map(lambda _: VMEM, outs) if out_specs is None else out_specs,
        scratch_shapes=list(scratch),
        compiler_params=pltpu.CompilerParams(vmem_limit_bytes=LIMIT),
    )


def rows_top():
    return lax.broadcasted_iota(jnp.int32, (8, LANES), 0) < 4


def swap(x):
    return pltpu.roll(x, LANES // 2, 1)


def turn(x):
    return pltpu.roll(x, 4, 0)


def split_cores(tiles):
    top = rows_top()
    low = [jnp.where(top, tiles[a], turn(tiles[a + 1])) for a in (0, 2)]
    high = [jnp.where(top, turn(tiles[a]), tiles[a + 1]) for a in (0, 2)]
    return jnp.concatenate(low, axis=0), jnp.concatenate(high, axis=0)


def pick(g, low, high):
    a, b = (rows[8 * (g // 2) : 8 * (g // 2) + 8] for rows in (low, high))
    return jnp.where(rows_top(), a, turn(b)) if g % 2 == 0 else jnp.where(rows_top(), turn(a), b)


def store_share(out_ref, z, term):
    for c in range(CORES):
        for k in range(SHARE):
            piece = term[16 * c : 16 * c + 16, k * LANES : (k + 1) * LANES]
            out_ref[CORES * z + c, 16 * k : 16 * k + 16, :] = piece.astype(BF16)


def load_share(in_ref, z):
    columns = []
    for m in range(PAIRS):
        pairs = [in_ref[SIDE * g + z, 16 * m : 16 * m + 16, :].astype(F32) for g in range(SIDE)]
        columns.append(jnp.concatenate(split_cores([p[:8] for p in pairs]), axis=0))
        columns.append(jnp.concatenate(split_cores([p[8:] for p in pairs]), axis=0))
    return jnp.concatenate(columns, axis=1).astype(BF16)


def spread_stats(place, shift, denom):
    lane = lax.broadcasted_iota(jnp.int32, (shift.shape[0], LANES), 1)
    high = denom.astype(BF16).astype(F32)
    stats = jnp.where(lane == place, shift, 0.0)
    stats = jnp.where(lane == place + SIDE, high, stats)
    return jnp.where(lane == place + 2 * SIDE, denom - high, stats)


def merge_stats(stats):
    valid = lax.broadcasted_iota(jnp.int32, stats.shape, 1) < SIDE
    largest = jnp.max(jnp.where(valid, stats, -jnp.inf), axis=1, keepdims=True)
    scale = jnp.exp(jnp.where(valid, stats - largest, 0.0))
    parts = pltpu.roll(stats, LANES - SIDE, 1) + pltpu.roll(stats, LANES - 2 * SIDE, 1)
    denom = jnp.sum(jnp.where(valid, scale * parts, 0.0), axis=1, keepdims=True)
    return largest, scale, denom


def key_kernel(key_ref, patch_ref, out_ref, spread_ref):
    del patch_ref
    for k in range(BLOCKS):
        spread_ref[k : k + 1, :] = key_ref[:, k * LANES : (k + 1) * LANES].astype(F32)
    block = spread_ref[...].astype(BF16)
    for e in range(EXP):
        out_ref[e] = block


def dispatch_kernel(place_ref, patch_ref, keys_ref, out_ref, combine_ref, spread_ref, table_ref):
    spread_ref[...] = keys_ref[...].astype(F32).reshape(EXP * BLOCKS, LANES)
    for k in range(BLOCKS):
        for c in range(CORES):
            rows = spread_ref[pl.ds(BLOCKS * c + k, 16, stride=CORES * BLOCKS), :]
            table_ref[16 * c : 16 * c + 16, k * LANES : (k + 1) * LANES] = rows.astype(BF16)
    logits = lax.dot_general(
        table_ref[...], patch_ref[0], (((1,), (1,)), ((), ())), preferred_element_type=F32
    )
    shift = jnp.max(logits, axis=1, keepdims=True).astype(BF16).astype(F32)
    raised = jnp.exp(logits - shift)
    denom = jnp.sum(raised, axis=1, keepdims=True)
    weights = raised.astype(BF16)
    rest = (raised - weights.astype(F32)).astype(BF16)
    weights = jnp.concatenate([weights, rest], axis=0)
    stats = spread_stats(place_ref[0], shift, denom)
    for z in range(SIDE):
        base = z * SHARE * LANES
        columns = patch_ref[0, :, base : base + SHARE * LANES]
        term = jnp.dot(weights, columns, preferred_element_type=F32)
        store_share(out_ref, z, term[:EXP] + term[EXP:])
        for c in range(CORES):
            both = stats[16 * c : 16 * c + 8] + swap(stats[16 * c + 8 : 16 * c + 16])
            out_ref[CORES * z + c, TALL : TALL + 8, :] = both.astype(BF16)
    raised = jnp.exp(logits - jnp.max(logits, axis=0, keepdims=True))
    combine = raised / jnp.sum(raised, axis=0, keepdims=True)
    combine_ref[...] = combine.T.astype(BF16)


def sum_near(in_ref, out_ref, factor):
    for m in range(PAIRS):
        sums = []
        for k in (2 * m, 2 * m + 1):
            for c in range(CORES):
                total = None
                for z in range(SIDE):
                    rows = in_ref[CORES * z + c, 16 * k : 16 * k + 16, :].astype(F32)
                    if factor is not None:
                        rows = factor[c][z] * rows
                    total = rows if z == 0 else total + rows
                sums.append(total)
        for g in range(SIDE):
            pair = [pick(g, sums[0], sums[1]), pick(g, sums[2], sums[3])]
            pair = jnp.concatenate(pair, axis=0).astype(BF16)
            for h in range(SIDE):
                out_ref[SIDE * g + h, 16 * m : 16 * m + 16, :] = pair


def merge_near_kernel(place_ref, in_ref, out_ref):
    gathered = []
    for c in range(CORES):
        total = in_ref[c, TALL : TALL + 8, :].astype(F32)
        for z in range(1, SIDE):
            total += in_ref[CORES * z + c, TALL : TALL + 8, :].astype(F32)
        gathered += [total, swap(total)]
    largest, scale, denom = merge_stats(jnp.concatenate(gathered, axis=0))
    factor = [
        [jnp.broadcast_to(scale[16 * c : 16 * c + 16, z : z + 1], (16, LANES)) for z in range(SIDE)]
        for c in range(CORES)
    ]
    sum_near(in_ref, out_ref, factor)
    stats = spread_stats(place_ref[0], largest, denom)
    for g in range(SIDE):
        tile = pick(g, stats[:16], stats[16:]).astype(BF16)
        for h in range(SIDE):
            out_ref[SIDE * g + h, WIDE : WIDE + 8, :] = tile


def add_near_kernel(in_ref, out_ref):
    sum_near(in_ref, out_ref, None)


def sum_far(in_ref, out_ref, spread_ref, factor):
    for m in range(PAIRS):
        lows, highs = [], []
        for g in range(SIDE):
            low = high = None
            for h in range(SIDE):
                pair = in_ref[SIDE * g + h, 16 * m : 16 * m + 16, :].astype(F32)
                a, b = pair[:8], pair[8:]
                if factor is not None:
                    a, b = factor[g][h] * a, factor[g][h] * b
                low, high = (a, b) if h == 0 else (low + a, high + b)
            lows.append(low)
            highs.append(high)
        spread_ref[64 * m : 64 * m + 32, :] = jnp.concatenate(split_cores(lows), axis=0)
        spread_ref[64 * m + 32 : 64 * m + 64, :] = jnp.concatenate(split_cores(highs), axis=0)
    for g in range(SIDE):
        for m in range(PAIRS):
            low = spread_ref[pl.ds(64 * m + g, 8, stride=SIDE), :]
            high = spread_ref[pl.ds(64 * m + 32 + g, 8, stride=SIDE), :]
            pair = jnp.concatenate([low, high], axis=0).astype(BF16)
            for z in range(SIDE):
                out_ref[SIDE * g + z, 16 * m : 16 * m + 16, :] = pair


def merge_far_kernel(in_ref, out_ref, spread_ref):
    gathered = []
    for g in range(SIDE):
        total = in_ref[SIDE * g, WIDE : WIDE + 8, :].astype(F32)
        for h in range(1, SIDE):
            total += in_ref[SIDE * g + h, WIDE : WIDE + 8, :].astype(F32)
        gathered.append(total)
    _, scale, denom = merge_stats(jnp.concatenate(gathered, axis=0))
    scale = scale / denom
    factor = [
        [jnp.broadcast_to(scale[8 * g : 8 * g + 8, h : h + 1], (8, LANES)) for h in range(SIDE)]
        for g in range(SIDE)
    ]
    sum_far(in_ref, out_ref, spread_ref, factor)


def add_far_kernel(in_ref, out_ref, spread_ref):
    sum_far(in_ref, out_ref, spread_ref, None)


def ffn_kernel(in_ref, first_ref, second_ref, out_ref):
    hidden = None
    for z in range(SIDE):
        base = z * SHARE * LANES
        term = lax.dot_general(
            load_share(in_ref, z),
            first_ref[0, :, base : base + SHARE * LANES],
            (((1,), (1,)), ((), ())),
            preferred_element_type=F32,
        )
        hidden = term if z == 0 else hidden + term
    activated = jax.nn.gelu(hidden).astype(BF16)
    for z in range(SIDE):
        base = z * SHARE * LANES
        columns = second_ref[0, :, base : base + SHARE * LANES]
        store_share(out_ref, z, jnp.dot(activated, columns, preferred_element_type=F32))


def mix_kernel(in_ref, combine_ref, out_ref, mixed_ref, sems):
    copies = []
    for z in range(SIDE):
        columns = slice(z * SHARE * LANES, (z + 1) * SHARE * LANES)
        mixed_ref[:, columns] = jnp.dot(
            combine_ref[...], load_share(in_ref, z), preferred_element_type=F32
        ).astype(BF16)
        copy = pltpu.make_async_copy(mixed_ref.at[:, columns], out_ref.at[0, :, columns], sems.at[z])
        copy.start()
        copies.append(copy)
    for copy in copies:
        copy.wait()


def exchange(x, *axes):
    return lax.all_to_all(x, axes, split_axis=0, concat_axis=0, tiled=True)


def shards(patches, slot_keys, w_in, w_out):
    rows = patches.shape[1]
    tall = sds((CORES * SIDE, TALL, LANES), BF16)
    tall_stats = sds((CORES * SIDE, TALL + 8, LANES), BF16)
    wide = sds((PEERS, WIDE, LANES), BF16)
    wide_stats = sds((PEERS, WIDE + 8, LANES), BF16)
    place_near = lax.axis_index("zl").astype(jnp.int32).reshape(1)
    place_far = lax.axis_index("zh").astype(jnp.int32).reshape(1)

    own_key = call(
        key_kernel,
        sds((EXP, BLOCKS, LANES), BF16),
        [VMEM, ANY],
        [pltpu.VMEM((BLOCKS, LANES), F32)],
    )(slot_keys, pltpu.with_memory_space_constraint(patches, pltpu.HBM))
    own_key, place_near, place_far = lax.optimization_barrier((own_key, place_near, place_far))
    keys = exchange(own_key, "x", "y", "core")
    terms, combine = call(
        dispatch_kernel,
        (tall_stats, sds((rows, EXP), BF16)),
        [SMEM, VMEM, VMEM],
        [pltpu.VMEM((EXP * BLOCKS, LANES), F32), pltpu.VMEM((EXP, D), BF16)],
    )(place_near, patches, keys)

    spread = [pltpu.VMEM((32 * SHARE, LANES), F32)]
    near = call(merge_near_kernel, wide_stats, [SMEM, VMEM])(place_far, exchange(terms, "zl", "core"))
    slot_tiles = call(merge_far_kernel, wide, [VMEM], spread)(exchange(near, "x", "zh"))
    out_terms = call(ffn_kernel, tall, [VMEM] * 3)(
        exchange(slot_tiles, "y", "zl"), jnp.swapaxes(w_in, 1, 2), w_out
    )
    near = call(add_near_kernel, wide, [VMEM])(exchange(out_terms, "zl", "core"))
    out_tiles = call(add_far_kernel, wide, [VMEM], spread)(exchange(near, "y", "zh"))
    return call(
        mix_kernel,
        sds((1, rows, D), BF16),
        [VMEM, VMEM],
        [pltpu.VMEM((rows, D), BF16), pltpu.SemaphoreType.DMA((SIDE,))],
        out_specs=ANY,
    )(exchange(out_tiles, "x", "zl"), combine)


def solution(mesh):
    split = Mesh(
        mesh.devices.reshape(SIDE, SIDE, SIDE, SIDE, CORES), ("zh", "zl", "x", "y", "core")
    )
    seq, exp = ("zh", "zl"), ("x", "y", "core")
    placed = (P(exp, seq, None), P(exp, None), P(exp, None, seq), P(exp, seq, None))
    return jax.shard_map(
        shards, mesh=split, in_specs=placed, out_specs=P(exp, seq, None), check_vma=False
    )
```

time: 130 us -> 126 us (0.969)
  blocking collectives: 123 us -> 119 us
    all_to_all x7, blocking collectives: 123 us -> 119 us  [exchange(): return lax.all_to_all(x, axes, split_axis=0, concat_axis=0, tiled=True)]
    pallas_call x6 -> x7, Pallas kernels: 2.97 us -> 3.01 us  [the longest x1 1.29 us: shards(): call(dispatch_kernel, (tall_stats, sds((rows, EXP), BF16)), [SMEM, VMEM,...]
where the time goes in v4:
time: 126 us; the launch traced here: 125 us
  blocking collectives  119 us (94%)
  Pallas kernels  4.38 us (3%)
    all_to_all x7, blocking collectives, exchange(): return lax.all_to_all(x, axes, split_axis=0, concat_axis=0, tiled=True)  119 us

profile of v4, /device:TPU:1, one launch (start us, length us, event | category | flops | bytes accessed | tf_op | source)
XLA Modules:
  0.0 124.6 jit_solution(10128913882164810299)
XLA Ops:
  0.0 0.0 copy-start
  0.0 0.0 copy-start.3
  0.0 0.8 copy-done.3
  0.8 17.9 %all_to_all.35.keys_ref = bf16[32,24,128]{2,1,0:T(8,128)(2,1)S(1)} all-to-all(bf16[32,24,128]{2,1,0:T(8,128)(2,1)S(1)} %shard_map.46), channel_id=1, replica_groups=mesh['zh'=4,'zl'=4,'x'=4,'y'=4,'core'=2] {'x','y','core'}, dimensions={0} | all-to-all | bytes 393216 | tf_op jit(solution)/shard_map/all_to_all | solution.py:254
  18.8 0.0 copy-done
  18.8 0.0 copy-start.2
  18.8 1.3 %shard_map.47 = (bf16[8,104,128]{2,1,0:T(8,128)(2,1)S(1)}, bf16[224,32]{1,0:T(8,128)(2,1)S(1)}) custom-call(s32[1]{0:T(128)} %bitcast.place_ref, bf16[1,224,3072]{2,1,0:T(8,128)(2,1)S(1)} %copy-done, bf16[32,24,128]{2,1,0:T(8,128)(2,1)S(1)} %all_to_all.35.keys_ref), custom_call_target="tpu_custom_call" | custom-call | tf_op jit(solution)/shard_map/pallas_call | solution.py:274
  20.1 0.0 copy-start.1
  20.1 11.6 %all_to_all.36.in_ref = bf16[8,104,128]{2,1,0:T(8,128)(2,1)S(1)} all-to-all(bf16[8,104,128]{2,1,0:T(8,128)(2,1)S(1)} %get-tuple-element.13), channel_id=1, replica_groups=mesh['zh'=4,'zl'=4,'x'=4,'y'=4,'core'=2] {'zl','core'}, dimensions={0} | all-to-all | bytes 425984 | tf_op jit(solution)/shard_map/all_to_all | solution.py:254
  31.7 0.3 shard_map.48
  32.0 32.1 %all_to_all.37.in_ref = bf16[16,56,128]{2,1,0:T(8,128)(2,1)S(1)} all-to-all(bf16[16,56,128]{2,1,0:T(8,128)(2,1)S(1)} %shard_map.48), channel_id=1, replica_groups=mesh['zh'=4,'zl'=4,'x'=4,'y'=4,'core'=2] {'x','zh'}, dimensions={0} | all-to-all | bytes 458752 | tf_op jit(solution)/shard_map/all_to_all | solution.py:254
  64.1 0.3 shard_map.49
  64.4 11.6 %all_to_all.38.in_ref = bf16[16,48,128]{2,1,0:T(8,128)(2,1)S(1)} all-to-all(bf16[16,48,128]{2,1,0:T(8,128)(2,1)S(1)} %shard_map.49), channel_id=1, replica_groups=mesh['zh'=4,'zl'=4,'x'=4,'y'=4,'core'=2] {'y','zl'}, dimensions={0} | all-to-all | bytes 393216 | tf_op jit(solution)/shard_map/all_to_all | solution.py:254
  76.0 0.0 copy-done.2
  76.0 0.0 copy-done.1
  76.0 1.0 shard_map.50
  77.0 12.8 %all_to_all.39.in_ref = bf16[8,96,128]{2,1,0:T(8,128)(2,1)S(1)} all-to-all(bf16[8,96,128]{2,1,0:T(8,128)(2,1)S(1)} %shard_map.50), channel_id=1, replica_groups=mesh['zh'=4,'zl'=4,'x'=4,'y'=4,'core'=2] {'zl','core'}, dimensions={0} | all-to-all | bytes 393216 | tf_op jit(solution)/shard_map/all_to_all | solution.py:254
  89.8 21.1 %all_to_all.40.in_ref = bf16[16,48,128]{2,1,0:T(8,128)(2,1)S(1)} all-to-all(bf16[16,48,128]{2,1,0:T(8,128)(2,1)S(1)} %shard_map.51), channel_id=1, replica_groups=mesh['zh'=4,'zl'=4,'x'=4,'y'=4,'core'=2] {'y','zh'}, dimensions={0} | all-to-all | bytes 393216 | tf_op jit(solution)/shard_map/all_to_all | solution.py:254
  111.0 12.3 %all_to_all.41.in_ref = bf16[16,48,128]{2,1,0:T(8,128)(2,1)S(1)} all-to-all(bf16[16,48,128]{2,1,0:T(8,128)(2,1)S(1)} %shard_map.52), channel_id=1, replica_groups=mesh['zh'=4,'zl'=4,'x'=4,'y'=4,'core'=2] {'x','zl'}, dimensions={0} | all-to-all | bytes 393216 | tf_op jit(solution)/shard_map/all_to_all | solution.py:254
  123.3 1.4 %shard_map.53 = bf16[1,224,3072]{2,1,0:T(8,128)(2,1)} custom-call(bf16[16,48,128]{2,1,0:T(8,128)(2,1)S(1)} %all_to_all.41.in_ref, bf16[224,32]{1,0:T(8,128)(2,1)S(1)} %get-tuple-element.14.combine_ref), custom_call_target="tpu_custom_call" | custom-call | tf_op jit(solution)/shard_map/pallas_call | solution.py:289
  (3 shorter events, 0.1 us)
Async XLA Ops:
  0.0 18.8 %copy-start = (bf16[1,224,3072]{2,1,0:T(8,128)(2,1)S(1)}, bf16[1,224,3072]{2,1,0:T(8,128)(2,1)}, u32[]{:S(2)}) copy-start(bf16[1,224,3072]{2,1,0:T(8,128)(2,1)} %patch_ref.3) | copy-start | bytes 4128772
  0.0 0.8 copy-start.3
  18.8 57.2 %copy-start.2 = (bf16[1,192,3072]{2,1,0:T(8,128)(2,1)S(1)}, bf16[1,192,3072]{2,1,0:T(8,128)(2,1)}, u32[]{:S(2)}) copy-start(bf16[1,192,3072]{2,1,0:T(8,128)(2,1)} %second_ref.1) | copy-start | bytes 3538948
  20.1 55.9 %copy-start.1 = (bf16[1,3072,192]{1,2,0:T(8,128)(2,1)S(1)}, bf16[1,3072,192]{1,2,0:T(8,128)(2,1)}, u32[]{:S(2)}) copy-start(bf16[1,3072,192]{1,2,0:T(8,128)(2,1)} %param.6) | copy-start | bytes 3538948

commit v5 on v4

--- a/solution.py
+++ b/solution.py
@@ -250,8 +250,31 @@
         copy.wait()
 
 
-def exchange(x, *axes):
-    return lax.all_to_all(x, axes, split_axis=0, concat_axis=0, tiled=True)
+def exchange(x, axes, groups=None):
+    return lax.all_to_all(x, axes, split_axis=0, concat_axis=0, tiled=True, axis_index_groups=groups)
+
+
+def column(h, z):
+    return (z + 2 * (h // 2)) % SIDE
+
+
+NEAR = [sorted((SIDE * h + z for z in range(SIDE)), key=lambda p: column(p // SIDE, p % SIDE)) for h in range(SIDE)]
+FAR = [[near[z] for near in NEAR] for z in range(SIDE)]
+
+
+def near_cores(x):
+    groups = [[CORES * z + c for z in near for c in range(CORES)] for near in NEAR]
+    return exchange(x, ("zh", "zl", "core"), groups)
+
+
+def far(x, axis):
+    groups = [[SIDE * z + g for g in range(SIDE) for z in far] for far in FAR]
+    return exchange(x, ("zh", "zl", axis), groups)
+
+
+def near(x, axis):
+    groups = [[SIDE * z + g for g in range(SIDE) for z in near] for near in NEAR]
+    return exchange(x, ("zh", "zl", axis), groups)
 
 
 def shards(patches, slot_keys, w_in, w_out):
@@ -260,8 +283,8 @@
     tall_stats = sds((CORES * SIDE, TALL + 8, LANES), BF16)
     wide = sds((PEERS, WIDE, LANES), BF16)
     wide_stats = sds((PEERS, WIDE + 8, LANES), BF16)
-    place_near = lax.axis_index("zl").astype(jnp.int32).reshape(1)
-    place_far = lax.axis_index("zh").astype(jnp.int32).reshape(1)
+    high, low = lax.axis_index("zh").astype(jnp.int32), lax.axis_index("zl").astype(jnp.int32)
+    place_near, place_far = column(high, low).reshape(1), high.reshape(1)
 
     own_key = call(
         key_kernel,
@@ -270,7 +293,7 @@
         [pltpu.VMEM((BLOCKS, LANES), F32)],
     )(slot_keys, pltpu.with_memory_space_constraint(patches, pltpu.HBM))
     own_key, place_near, place_far = lax.optimization_barrier((own_key, place_near, place_far))
-    keys = exchange(own_key, "x", "y", "core")
+    keys = exchange(own_key, ("x", "y", "core"))
     terms, combine = call(
         dispatch_kernel,
         (tall_stats, sds((rows, EXP), BF16)),
@@ -279,20 +302,20 @@
     )(place_near, patches, keys)
 
     spread = [pltpu.VMEM((32 * SHARE, LANES), F32)]
-    near = call(merge_near_kernel, wide_stats, [SMEM, VMEM])(place_far, exchange(terms, "zl", "core"))
-    slot_tiles = call(merge_far_kernel, wide, [VMEM], spread)(exchange(near, "x", "zh"))
+    parts = call(merge_near_kernel, wide_stats, [SMEM, VMEM])(place_far, near_cores(terms))
+    slot_tiles = call(merge_far_kernel, wide, [VMEM], spread)(far(parts, "x"))
     out_terms = call(ffn_kernel, tall, [VMEM] * 3)(
-        exchange(slot_tiles, "y", "zl"), jnp.swapaxes(w_in, 1, 2), w_out
-    )
-    near = call(add_near_kernel, wide, [VMEM])(exchange(out_terms, "zl", "core"))
-    out_tiles = call(add_far_kernel, wide, [VMEM], spread)(exchange(near, "y", "zh"))
+        near(slot_tiles, "y"), jnp.swapaxes(w_in, 1, 2), w_out
+    )
+    parts = call(add_near_kernel, wide, [VMEM])(near_cores(out_terms))
+    out_tiles = call(add_far_kernel, wide, [VMEM], spread)(far(parts, "y"))
     return call(
         mix_kernel,
         sds((1, rows, D), BF16),
         [VMEM, VMEM],
         [pltpu.VMEM((rows, D), BF16), pltpu.SemaphoreType.DMA((SIDE,))],
         out_specs=ANY,
-    )(exchange(out_tiles, "x", "zl"), combine)
+    )(near(out_tiles, "x"), combine)
 
 
 def solution(mesh):

time: 126 us -> 122 us (0.968)
  blocking collectives: 119 us -> 116 us
    all_to_all x7, blocking collectives: 119 us -> 116 us  [exchange(): lax.all_to_all(x, axes, split_axis=0, concat_axis=0, tiled=True, axis_ind...]
where the time goes in v5:
time: 122 us
  blocking collectives  116 us (95%)
  Pallas kernels  4.38 us (4%)
    all_to_all x7, blocking collectives, exchange(): lax.all_to_all(x, axes, split_axis=0, concat_axis=0, tiled=True, axis_ind...  116 us

profile of v5, /device:TPU:1, one launch (start us, length us, event | category | flops | bytes accessed | tf_op | source)
XLA Modules:
  0.0 121.7 jit_solution(15633881716611380953)
XLA Ops:
  0.0 0.0 copy-start
  0.0 0.0 copy-start.3
  0.0 0.8 copy-done.3
  0.8 17.9 %all_to_all.35.keys_ref = bf16[32,24,128]{2,1,0:T(8,128)(2,1)S(1)} all-to-all(bf16[32,24,128]{2,1,0:T(8,128)(2,1)S(1)} %shard_map.46), channel_id=1, replica_groups=mesh['zh'=4,'zl'=4,'x'=4,'y'=4,'core'=2] {'x','y','core'}, dimensions={0} | all-to-all | bytes 393216 | tf_op jit(solution)/shard_map/all_to_all | solution.py:254
  18.8 0.0 copy-done
  18.8 0.0 copy-start.2
  18.8 1.3 %shard_map.47 = (bf16[8,104,128]{2,1,0:T(8,128)(2,1)S(1)}, bf16[224,32]{1,0:T(8,128)(2,1)S(1)}) custom-call(s32[1]{0:T(128)} %bitcast.place_ref, bf16[1,224,3072]{2,1,0:T(8,128)(2,1)S(1)} %copy-done, bf16[32,24,128]{2,1,0:T(8,128)(2,1)S(1)} %all_to_all.35.keys_ref), custom_call_target="tpu_custom_call" | custom-call | tf_op jit(solution)/shard_map/pallas_call | solution.py:297
  20.1 0.0 copy-start.1
  20.1 11.6 %all_to_all.36.in_ref = bf16[8,104,128]{2,1,0:T(8,128)(2,1)S(1)} all-to-all(bf16[8,104,128]{2,1,0:T(8,128)(2,1)S(1)} %get-tuple-element.13), channel_id=1, replica_groups={{0,1,32,33,64,65,96,97},{128,129,160,161,192,193,224,225},{320,321,352,..., dimensions={0} | all-to-all | bytes 425984 | tf_op jit(solution)/shard_map/all_to_all | solution.py:254
  31.7 0.3 shard_map.48
  32.0 31.3 %all_to_all.37.in_ref = bf16[16,56,128]{2,1,0:T(8,128)(2,1)S(1)} all-to-all(bf16[16,56,128]{2,1,0:T(8,128)(2,1)S(1)} %shard_map.48), channel_id=1, replica_groups={{0,128,320,448,8,136,328,456,16,144,336,464,24,152,344,472},{32,160,352..., dimensions={0} | all-to-all | bytes 458752 | tf_op jit(solution)/shard_map/all_to_all | solution.py:254
  63.3 0.3 shard_map.49
  63.6 10.1 %all_to_all.38.in_ref = bf16[16,48,128]{2,1,0:T(8,128)(2,1)S(1)} all-to-all(bf16[16,48,128]{2,1,0:T(8,128)(2,1)S(1)} %shard_map.49), channel_id=1, replica_groups={{0,32,64,96,2,34,66,98,4,36,68,100,6,38,70,102},{128,160,192,224,130,16..., dimensions={0} | all-to-all | bytes 393216 | tf_op jit(solution)/shard_map/all_to_all | solution.py:254
  73.7 0.0 copy-done.2
  73.7 0.0 copy-done.1
  73.7 1.0 shard_map.50
  74.7 12.0 %all_to_all.39.in_ref = bf16[8,96,128]{2,1,0:T(8,128)(2,1)S(1)} all-to-all(bf16[8,96,128]{2,1,0:T(8,128)(2,1)S(1)} %shard_map.50), channel_id=1, replica_groups={{0,1,32,33,64,65,96,97},{128,129,160,161,192,193,224,225},{320,321,352,..., dimensions={0} | all-to-all | bytes 393216 | tf_op jit(solution)/shard_map/all_to_all | solution.py:254
  86.8 20.8 %all_to_all.40.in_ref = bf16[16,48,128]{2,1,0:T(8,128)(2,1)S(1)} all-to-all(bf16[16,48,128]{2,1,0:T(8,128)(2,1)S(1)} %shard_map.51), channel_id=1, replica_groups={{0,128,320,448,2,130,322,450,4,132,324,452,6,134,326,454},{32,160,352,4..., dimensions={0} | all-to-all | bytes 393216 | tf_op jit(solution)/shard_map/all_to_all | solution.py:254
  107.6 12.7 %all_to_all.41.in_ref = bf16[16,48,128]{2,1,0:T(8,128)(2,1)S(1)} all-to-all(bf16[16,48,128]{2,1,0:T(8,128)(2,1)S(1)} %shard_map.52), channel_id=1, replica_groups={{0,32,64,96,8,40,72,104,16,48,80,112,24,56,88,120},{128,160,192,224,136..., dimensions={0} | all-to-all | bytes 393216 | tf_op jit(solution)/shard_map/all_to_all | solution.py:254
  120.3 1.4 %shard_map.53 = bf16[1,224,3072]{2,1,0:T(8,128)(2,1)} custom-call(bf16[16,48,128]{2,1,0:T(8,128)(2,1)S(1)} %all_to_all.41.in_ref, bf16[224,32]{1,0:T(8,128)(2,1)S(1)} %get-tuple-element.14.combine_ref), custom_call_target="tpu_custom_call" | custom-call | tf_op jit(solution)/shard_map/pallas_call | solution.py:312
  (3 shorter events, 0.1 us)
Async XLA Ops:
  0.0 18.8 %copy-start = (bf16[1,224,3072]{2,1,0:T(8,128)(2,1)S(1)}, bf16[1,224,3072]{2,1,0:T(8,128)(2,1)}, u32[]{:S(2)}) copy-start(bf16[1,224,3072]{2,1,0:T(8,128)(2,1)} %patch_ref.3) | copy-start | bytes 4128772
  0.0 0.8 copy-start.3
  18.8 54.9 %copy-start.2 = (bf16[1,192,3072]{2,1,0:T(8,128)(2,1)S(1)}, bf16[1,192,3072]{2,1,0:T(8,128)(2,1)}, u32[]{:S(2)}) copy-start(bf16[1,192,3072]{2,1,0:T(8,128)(2,1)} %second_ref.1) | copy-start | bytes 3538948
  20.1 53.6 %copy-start.1 = (bf16[1,3072,192]{1,2,0:T(8,128)(2,1)S(1)}, bf16[1,3072,192]{1,2,0:T(8,128)(2,1)}, u32[]{:S(2)}) copy-start(bf16[1,3072,192]{1,2,0:T(8,128)(2,1)} %param.6) | copy-start | bytes 3538948

commit v6 on v5

--- a/solution.py
+++ b/solution.py
@@ -19,9 +19,9 @@
 TALL = 16 * SHARE
 WIDE = 8 * SHARE
 VMEM = pl.BlockSpec(memory_space=pltpu.VMEM)
-SMEM = pl.BlockSpec(memory_space=pltpu.SMEM)
 ANY = pl.BlockSpec(memory_space=pl.ANY)
 LIMIT = 24 * 1024 * 1024
+GROUP = 16
 sds = jax.ShapeDtypeStruct
 
 
@@ -76,21 +76,24 @@
     return jnp.concatenate(columns, axis=1).astype(BF16)
 
 
-def spread_stats(place, shift, denom):
-    lane = lax.broadcasted_iota(jnp.int32, (shift.shape[0], LANES), 1)
-    high = denom.astype(BF16).astype(F32)
-    stats = jnp.where(lane == place, shift, 0.0)
-    stats = jnp.where(lane == place + SIDE, high, stats)
-    return jnp.where(lane == place + 2 * SIDE, denom - high, stats)
-
-
-def merge_stats(stats):
-    valid = lax.broadcasted_iota(jnp.int32, stats.shape, 1) < SIDE
-    largest = jnp.max(jnp.where(valid, stats, -jnp.inf), axis=1, keepdims=True)
-    scale = jnp.exp(jnp.where(valid, stats - largest, 0.0))
-    parts = pltpu.roll(stats, LANES - SIDE, 1) + pltpu.roll(stats, LANES - 2 * SIDE, 1)
-    denom = jnp.sum(jnp.where(valid, scale * parts, 0.0), axis=1, keepdims=True)
-    return largest, scale, denom
+def lane_groups(rows):
+    return lax.broadcasted_iota(jnp.int32, (rows, LANES), 1) % (LANES // 2) // GROUP
+
+
+def join_stats(shift, high, rest):
+    group = lane_groups(shift.shape[0])
+    return jnp.where(group == 0, shift, jnp.where(group == 1, high, jnp.where(group == 2, rest, 0.0)))
+
+
+def merge_stats(tiles):
+    largest = jnp.maximum(jnp.maximum(tiles[0], tiles[1]), jnp.maximum(tiles[2], tiles[3]))
+    scale = [jnp.exp(t - largest) for t in tiles]
+    parts = [pltpu.roll(f, GROUP, 1) * (t + pltpu.roll(t, LANES - GROUP, 1)) for f, t in zip(scale, tiles)]
+    return largest, scale, parts[0] + parts[1] + parts[2] + parts[3]
+
+
+def all_lanes(x, lane):
+    return jnp.broadcast_to(x[:, lane : lane + 1], x.shape)
 
 
 def key_kernel(key_ref, patch_ref, out_ref, spread_ref):
@@ -102,22 +105,37 @@
         out_ref[e] = block
 
 
-def dispatch_kernel(place_ref, patch_ref, keys_ref, out_ref, combine_ref, spread_ref, table_ref):
+def dispatch_kernel(patch_ref, keys_ref, out_ref, combine_ref, spread_ref, table_ref):
     spread_ref[...] = keys_ref[...].astype(F32).reshape(EXP * BLOCKS, LANES)
     for k in range(BLOCKS):
         for c in range(CORES):
             rows = spread_ref[pl.ds(BLOCKS * c + k, 16, stride=CORES * BLOCKS), :]
             table_ref[16 * c : 16 * c + 16, k * LANES : (k + 1) * LANES] = rows.astype(BF16)
-    logits = lax.dot_general(
-        table_ref[...], patch_ref[0], (((1,), (1,)), ((), ())), preferred_element_type=F32
-    )
+    half, deep = patch_ref.shape[1] // 2, D // 2
+    logits = jnp.concatenate(
+        [
+            sum(
+                lax.dot_general(
+                    patch_ref[0, i * half : (i + 1) * half, k * deep : (k + 1) * deep],
+                    table_ref[:, k * deep : (k + 1) * deep],
+                    (((1,), (1,)), ((), ())),
+                    preferred_element_type=F32,
+                )
+                for k in range(2)
+            )
+            for i in range(2)
+        ],
+        axis=0,
+    ).T
     shift = jnp.max(logits, axis=1, keepdims=True).astype(BF16).astype(F32)
     raised = jnp.exp(logits - shift)
     denom = jnp.sum(raised, axis=1, keepdims=True)
     weights = raised.astype(BF16)
     rest = (raised - weights.astype(F32)).astype(BF16)
     weights = jnp.concatenate([weights, rest], axis=0)
-    stats = spread_stats(place_ref[0], shift, denom)
+    high = denom.astype(BF16).astype(F32)
+    left = lax.broadcasted_iota(jnp.int32, (EXP, LANES), 1) < LANES // 2
+    stats = jnp.where(left, join_stats(shift, high, denom - high), 0.0)
     for z in range(SIDE):
         base = z * SHARE * LANES
         columns = patch_ref[0, :, base : base + SHARE * LANES]
@@ -150,22 +168,18 @@
                 out_ref[SIDE * g + h, 16 * m : 16 * m + 16, :] = pair
 
 
-def merge_near_kernel(place_ref, in_ref, out_ref):
-    gathered = []
+def merge_near_kernel(in_ref, out_ref):
+    factor, stats = [], []
     for c in range(CORES):
-        total = in_ref[c, TALL : TALL + 8, :].astype(F32)
-        for z in range(1, SIDE):
-            total += in_ref[CORES * z + c, TALL : TALL + 8, :].astype(F32)
-        gathered += [total, swap(total)]
-    largest, scale, denom = merge_stats(jnp.concatenate(gathered, axis=0))
-    factor = [
-        [jnp.broadcast_to(scale[16 * c : 16 * c + 16, z : z + 1], (16, LANES)) for z in range(SIDE)]
-        for c in range(CORES)
-    ]
+        tiles = [in_ref[CORES * z + c, TALL : TALL + 8, :].astype(F32) for z in range(SIDE)]
+        largest, scale, denom = merge_stats(tiles)
+        factor.append([jnp.concatenate([all_lanes(f, 0), all_lanes(f, LANES // 2)], axis=0) for f in scale])
+        high = denom.astype(BF16).astype(F32)
+        joined = join_stats(largest, high, pltpu.roll(denom - high, GROUP, 1))
+        stats.append(jnp.concatenate([joined, swap(joined)], axis=0))
     sum_near(in_ref, out_ref, factor)
-    stats = spread_stats(place_ref[0], largest, denom)
     for g in range(SIDE):
-        tile = pick(g, stats[:16], stats[16:]).astype(BF16)
+        tile = pick(g, stats[0], stats[1]).astype(BF16)
         for h in range(SIDE):
             out_ref[SIDE * g + h, WIDE : WIDE + 8, :] = tile
 
@@ -199,18 +213,12 @@
 
 
 def merge_far_kernel(in_ref, out_ref, spread_ref):
-    gathered = []
+    factor = []
     for g in range(SIDE):
-        total = in_ref[SIDE * g, WIDE : WIDE + 8, :].astype(F32)
-        for h in range(1, SIDE):
-            total += in_ref[SIDE * g + h, WIDE : WIDE + 8, :].astype(F32)
-        gathered.append(total)
-    _, scale, denom = merge_stats(jnp.concatenate(gathered, axis=0))
-    scale = scale / denom
-    factor = [
-        [jnp.broadcast_to(scale[8 * g : 8 * g + 8, h : h + 1], (8, LANES)) for h in range(SIDE)]
-        for g in range(SIDE)
-    ]
+        tiles = [in_ref[SIDE * g + h, WIDE : WIDE + 8, :].astype(F32) for h in range(SIDE)]
+        _, scale, denom = merge_stats(tiles)
+        inverse = pltpu.roll(1.0 / denom, LANES - GROUP, 1)
+        factor.append([all_lanes(f * inverse, 0) for f in scale])
     sum_far(in_ref, out_ref, spread_ref, factor)
 
 
@@ -220,15 +228,20 @@
 
 def ffn_kernel(in_ref, first_ref, second_ref, out_ref):
     hidden = None
-    for z in range(SIDE):
-        base = z * SHARE * LANES
-        term = lax.dot_general(
-            load_share(in_ref, z),
-            first_ref[0, :, base : base + SHARE * LANES],
-            (((1,), (1,)), ((), ())),
-            preferred_element_type=F32,
-        )
-        hidden = term if z == 0 else hidden + term
+    part = first_ref.shape[1] // 4
+    for k in range(2):
+        rows = jnp.concatenate([load_share(in_ref, 2 * k), load_share(in_ref, 2 * k + 1)], axis=1)
+        terms = [
+            lax.dot_general(
+                rows,
+                first_ref[0, i * part : (i + 1) * part, k * D // 2 : (k + 1) * D // 2],
+                (((1,), (1,)), ((), ())),
+                preferred_element_type=F32,
+            )
+            for i in range(4)
+        ]
+        term = jnp.concatenate(terms, axis=1)
+        hidden = term if k == 0 else hidden + term
     activated = jax.nn.gelu(hidden).astype(BF16)
     for z in range(SIDE):
         base = z * SHARE * LANES
@@ -283,8 +296,6 @@
     tall_stats = sds((CORES * SIDE, TALL + 8, LANES), BF16)
     wide = sds((PEERS, WIDE, LANES), BF16)
     wide_stats = sds((PEERS, WIDE + 8, LANES), BF16)
-    high, low = lax.axis_index("zh").astype(jnp.int32), lax.axis_index("zl").astype(jnp.int32)
-    place_near, place_far = column(high, low).reshape(1), high.reshape(1)
 
     own_key = call(
         key_kernel,
@@ -292,17 +303,16 @@
         [VMEM, ANY],
         [pltpu.VMEM((BLOCKS, LANES), F32)],
     )(slot_keys, pltpu.with_memory_space_constraint(patches, pltpu.HBM))
-    own_key, place_near, place_far = lax.optimization_barrier((own_key, place_near, place_far))
     keys = exchange(own_key, ("x", "y", "core"))
     terms, combine = call(
         dispatch_kernel,
         (tall_stats, sds((rows, EXP), BF16)),
-        [SMEM, VMEM, VMEM],
+        [VMEM, VMEM],
         [pltpu.VMEM((EXP * BLOCKS, LANES), F32), pltpu.VMEM((EXP, D), BF16)],
-    )(place_near, patches, keys)
+    )(patches, keys)
 
     spread = [pltpu.VMEM((32 * SHARE, LANES), F32)]
-    parts = call(merge_near_kernel, wide_stats, [SMEM, VMEM])(place_far, near_cores(terms))
+    parts = call(merge_near_kernel, wide_stats, [VMEM])(near_cores(terms))
     slot_tiles = call(merge_far_kernel, wide, [VMEM], spread)(far(parts, "x"))
     out_terms = call(ffn_kernel, tall, [VMEM] * 3)(
         near(slot_tiles, "y"), jnp.swapaxes(w_in, 1, 2), w_out

time: 122 us -> 122 us (level)
  no operation moved by 1% of the time
where the time goes in v6:
time: 122 us; the launch traced here: 121 us
  blocking collectives  116 us (95%)
  Pallas kernels  3.81 us (3%)
    all_to_all x7, blocking collectives, exchange(): lax.all_to_all(x, axes, split_axis=0, concat_axis=0, tiled=True, axis_ind...  116 us

profile of v6, /device:TPU:1, one launch (start us, length us, event | category | flops | bytes accessed | tf_op | source)
XLA Modules:
  0.0 121.2 jit_solution(14398864818005159749)
XLA Ops:
  0.0 0.0 copy-start
  0.0 0.0 copy-start.3
  0.0 0.8 copy-done.3
  0.8 17.9 %all_to_all.35.keys_ref = bf16[32,24,128]{2,1,0:T(8,128)(2,1)S(1)} all-to-all(bf16[32,24,128]{2,1,0:T(8,128)(2,1)S(1)} %shard_map.46), channel_id=1, replica_groups=mesh['zh'=4,'zl'=4,'x'=4,'y'=4,'core'=2] {'x','y','core'}, dimensions={0} | all-to-all | bytes 393216 | tf_op jit(solution)/shard_map/all_to_all | solution.py:267
  18.8 0.0 copy-done
  18.8 0.0 copy-start.2
  18.8 1.0 shard_map.47
  19.8 0.0 copy-start.1
  19.8 11.6 %all_to_all.36.in_ref = bf16[8,104,128]{2,1,0:T(8,128)(2,1)S(1)} all-to-all(bf16[8,104,128]{2,1,0:T(8,128)(2,1)S(1)} %get-tuple-element.7), channel_id=1, replica_groups={{0,1,32,33,64,65,96,97},{128,129,160,161,192,193,224,225},{320,321,352,..., dimensions={0} | all-to-all | bytes 425984 | tf_op jit(solution)/shard_map/all_to_all | solution.py:267
  31.4 0.2 shard_map.48
  31.6 31.3 %all_to_all.37.in_ref = bf16[16,56,128]{2,1,0:T(8,128)(2,1)S(1)} all-to-all(bf16[16,56,128]{2,1,0:T(8,128)(2,1)S(1)} %shard_map.48), channel_id=1, replica_groups={{0,128,320,448,8,136,328,456,16,144,336,464,24,152,344,472},{32,160,352..., dimensions={0} | all-to-all | bytes 458752 | tf_op jit(solution)/shard_map/all_to_all | solution.py:267
  62.9 0.3 shard_map.49
  63.2 10.1 %all_to_all.38.in_ref = bf16[16,48,128]{2,1,0:T(8,128)(2,1)S(1)} all-to-all(bf16[16,48,128]{2,1,0:T(8,128)(2,1)S(1)} %shard_map.49), channel_id=1, replica_groups={{0,32,64,96,2,34,66,98,4,36,68,100,6,38,70,102},{128,160,192,224,130,16..., dimensions={0} | all-to-all | bytes 393216 | tf_op jit(solution)/shard_map/all_to_all | solution.py:267
  73.3 0.0 copy-done.2
  73.3 0.0 copy-done.1
  73.3 0.8 shard_map.50
  74.1 12.1 %all_to_all.39.in_ref = bf16[8,96,128]{2,1,0:T(8,128)(2,1)S(1)} all-to-all(bf16[8,96,128]{2,1,0:T(8,128)(2,1)S(1)} %shard_map.50), channel_id=1, replica_groups={{0,1,32,33,64,65,96,97},{128,129,160,161,192,193,224,225},{320,321,352,..., dimensions={0} | all-to-all | bytes 393216 | tf_op jit(solution)/shard_map/all_to_all | solution.py:267
  86.2 20.8 %all_to_all.40.in_ref = bf16[16,48,128]{2,1,0:T(8,128)(2,1)S(1)} all-to-all(bf16[16,48,128]{2,1,0:T(8,128)(2,1)S(1)} %shard_map.51), channel_id=1, replica_groups={{0,128,320,448,2,130,322,450,4,132,324,452,6,134,326,454},{32,160,352,4..., dimensions={0} | all-to-all | bytes 393216 | tf_op jit(solution)/shard_map/all_to_all | solution.py:267
  107.1 12.7 %all_to_all.41.in_ref = bf16[16,48,128]{2,1,0:T(8,128)(2,1)S(1)} all-to-all(bf16[16,48,128]{2,1,0:T(8,128)(2,1)S(1)} %shard_map.52), channel_id=1, replica_groups={{0,32,64,96,8,40,72,104,16,48,80,112,24,56,88,120},{128,160,192,224,136..., dimensions={0} | all-to-all | bytes 393216 | tf_op jit(solution)/shard_map/all_to_all | solution.py:267
  119.8 1.4 %shard_map.53 = bf16[1,224,3072]{2,1,0:T(8,128)(2,1)} custom-call(bf16[16,48,128]{2,1,0:T(8,128)(2,1)S(1)} %all_to_all.41.in_ref, bf16[224,32]{1,0:T(8,128)(2,1)S(1)} %get-tuple-element.8.combine_ref), custom_call_target="tpu_custom_call" | custom-call | tf_op jit(solution)/shard_map/pallas_call | solution.py:322
  (3 shorter events, 0.1 us)
Async XLA Ops:
  0.0 18.8 %copy-start = (bf16[1,224,3072]{2,1,0:T(8,128)(2,1)S(1)}, bf16[1,224,3072]{2,1,0:T(8,128)(2,1)}, u32[]{:S(2)}) copy-start(bf16[1,224,3072]{2,1,0:T(8,128)(2,1)} %patch_ref.3) | copy-start | bytes 4128772
  0.0 0.8 copy-start.3
  18.8 54.5 %copy-start.2 = (bf16[1,192,3072]{2,1,0:T(8,128)(2,1)S(1)}, bf16[1,192,3072]{2,1,0:T(8,128)(2,1)}, u32[]{:S(2)}) copy-start(bf16[1,192,3072]{2,1,0:T(8,128)(2,1)} %second_ref.1) | copy-start | bytes 3538948
  19.8 53.5 %copy-start.1 = (bf16[1,3072,192]{1,2,0:T(8,128)(2,1)S(1)}, bf16[1,3072,192]{1,2,0:T(8,128)(2,1)}, u32[]{:S(2)}) copy-start(bf16[1,3072,192]{1,2,0:T(8,128)(2,1)} %param.6) | copy-start | bytes 3538948

commit v7 on v6

--- a/solution.py
+++ b/solution.py
@@ -18,6 +18,7 @@
 PEERS = SIDE * SIDE
 TALL = 16 * SHARE
 WIDE = 8 * SHARE
+FLAT = (CORES * SHARE + 1) * LANES
 VMEM = pl.BlockSpec(memory_space=pltpu.VMEM)
 ANY = pl.BlockSpec(memory_space=pl.ANY)
 LIMIT = 24 * 1024 * 1024
@@ -149,23 +150,14 @@
     combine_ref[...] = combine.T.astype(BF16)
 
 
-def sum_near(in_ref, out_ref, factor):
-    for m in range(PAIRS):
-        sums = []
-        for k in (2 * m, 2 * m + 1):
-            for c in range(CORES):
-                total = None
-                for z in range(SIDE):
-                    rows = in_ref[CORES * z + c, 16 * k : 16 * k + 16, :].astype(F32)
-                    if factor is not None:
-                        rows = factor[c][z] * rows
-                    total = rows if z == 0 else total + rows
-                sums.append(total)
-        for g in range(SIDE):
-            pair = [pick(g, sums[0], sums[1]), pick(g, sums[2], sums[3])]
-            pair = jnp.concatenate(pair, axis=0).astype(BF16)
-            for h in range(SIDE):
-                out_ref[SIDE * g + h, 16 * m : 16 * m + 16, :] = pair
+def near_total(in_ref, c, k, factor):
+    total = None
+    for z in range(SIDE):
+        rows = in_ref[CORES * z + c, 16 * k : 16 * k + 16, :].astype(F32)
+        if factor is not None:
+            rows = factor[c][z] * rows
+        total = rows if z == 0 else total + rows
+    return total
 
 
 def merge_near_kernel(in_ref, out_ref):
@@ -177,32 +169,31 @@
         high = denom.astype(BF16).astype(F32)
         joined = join_stats(largest, high, pltpu.roll(denom - high, GROUP, 1))
         stats.append(jnp.concatenate([joined, swap(joined)], axis=0))
-    sum_near(in_ref, out_ref, factor)
+    for k in range(SHARE):
+        for c in range(CORES):
+            total = near_total(in_ref, c, k, factor).astype(BF16)
+            lanes = slice((CORES * k + c) * LANES, (CORES * k + c + 1) * LANES)
+            for g in range(SIDE):
+                for h in range(SIDE):
+                    out_ref[SIDE * g + h, :, lanes] = total[4 * g : 4 * g + 4]
+    left = lax.broadcasted_iota(jnp.int32, (16, LANES), 1) < LANES // 2
+    both = jnp.where(left, stats[0], swap(stats[1])).astype(BF16)
     for g in range(SIDE):
-        tile = pick(g, stats[0], stats[1]).astype(BF16)
         for h in range(SIDE):
-            out_ref[SIDE * g + h, WIDE : WIDE + 8, :] = tile
+            out_ref[SIDE * g + h, :, FLAT - LANES :] = both[4 * g : 4 * g + 4]
 
 
 def add_near_kernel(in_ref, out_ref):
-    sum_near(in_ref, out_ref, None)
-
-
-def sum_far(in_ref, out_ref, spread_ref, factor):
     for m in range(PAIRS):
-        lows, highs = [], []
+        sums = [near_total(in_ref, c, k, None) for k in (2 * m, 2 * m + 1) for c in range(CORES)]
         for g in range(SIDE):
-            low = high = None
+            pair = [pick(g, sums[0], sums[1]), pick(g, sums[2], sums[3])]
+            pair = jnp.concatenate(pair, axis=0).astype(BF16)
             for h in range(SIDE):
-                pair = in_ref[SIDE * g + h, 16 * m : 16 * m + 16, :].astype(F32)
-                a, b = pair[:8], pair[8:]
-                if factor is not None:
-                    a, b = factor[g][h] * a, factor[g][h] * b
-                low, high = (a, b) if h == 0 else (low + a, high + b)
-            lows.append(low)
-            highs.append(high)
-        spread_ref[64 * m : 64 * m + 32, :] = jnp.concatenate(split_cores(lows), axis=0)
-        spread_ref[64 * m + 32 : 64 * m + 64, :] = jnp.concatenate(split_cores(highs), axis=0)
+                out_ref[SIDE * g + h, 16 * m : 16 * m + 16, :] = pair
+
+
+def store_turned(out_ref, spread_ref):
     for g in range(SIDE):
         for m in range(PAIRS):
             low = spread_ref[pl.ds(64 * m + g, 8, stride=SIDE), :]
@@ -215,15 +206,35 @@
 def merge_far_kernel(in_ref, out_ref, spread_ref):
     factor = []
     for g in range(SIDE):
-        tiles = [in_ref[SIDE * g + h, WIDE : WIDE + 8, :].astype(F32) for h in range(SIDE)]
+        tiles = [in_ref[SIDE * g + h, :, FLAT - LANES :].astype(F32) for h in range(SIDE)]
         _, scale, denom = merge_stats(tiles)
         inverse = pltpu.roll(1.0 / denom, LANES - GROUP, 1)
-        factor.append([all_lanes(f * inverse, 0) for f in scale])
-    sum_far(in_ref, out_ref, spread_ref, factor)
+        scale = [f * inverse for f in scale]
+        factor.append([[all_lanes(f, c * (LANES // 2)) for f in scale] for c in range(CORES)])
+    for k in range(SHARE):
+        for c in range(CORES):
+            lanes = slice((CORES * k + c) * LANES, (CORES * k + c + 1) * LANES)
+            for g in range(SIDE):
+                total = None
+                for h in range(SIDE):
+                    rows = factor[g][c][h] * in_ref[SIDE * g + h, :, lanes].astype(F32)
+                    total = rows if h == 0 else total + rows
+                first = 32 * k + 16 * c + 4 * g
+                spread_ref[first : first + 4, :] = total
+    store_turned(out_ref, spread_ref)
 
 
 def add_far_kernel(in_ref, out_ref, spread_ref):
-    sum_far(in_ref, out_ref, spread_ref, None)
+    for m in range(PAIRS):
+        lows, highs = [], []
+        for g in range(SIDE):
+            pairs = [in_ref[SIDE * g + h, 16 * m : 16 * m + 16, :].astype(F32) for h in range(SIDE)]
+            total = pairs[0] + pairs[1] + pairs[2] + pairs[3]
+            lows.append(total[:8])
+            highs.append(total[8:])
+        spread_ref[64 * m : 64 * m + 32, :] = jnp.concatenate(split_cores(lows), axis=0)
+        spread_ref[64 * m + 32 : 64 * m + 64, :] = jnp.concatenate(split_cores(highs), axis=0)
+    store_turned(out_ref, spread_ref)
 
 
 def ffn_kernel(in_ref, first_ref, second_ref, out_ref):
@@ -295,7 +306,7 @@
     tall = sds((CORES * SIDE, TALL, LANES), BF16)
     tall_stats = sds((CORES * SIDE, TALL + 8, LANES), BF16)
     wide = sds((PEERS, WIDE, LANES), BF16)
-    wide_stats = sds((PEERS, WIDE + 8, LANES), BF16)
+    flat_stats = sds((PEERS, 4, FLAT), BF16)
 
     own_key = call(
         key_kernel,
@@ -312,7 +323,7 @@
     )(patches, keys)
 
     spread = [pltpu.VMEM((32 * SHARE, LANES), F32)]
-    parts = call(merge_near_kernel, wide_stats, [VMEM])(near_cores(terms))
+    parts = call(merge_near_kernel, flat_stats, [VMEM])(near_cores(terms))
     slot_tiles = call(merge_far_kernel, wide, [VMEM], spread)(far(parts, "x"))
     out_terms = call(ffn_kernel, tall, [VMEM] * 3)(
         near(slot_tiles, "y"), jnp.swapaxes(w_in, 1, 2), w_out

time: 122 us -> 121 us (level)
  no operation moved by 1% of the time
where the time goes in v7:
time: 121 us
  blocking collectives  116 us (96%)
  Pallas kernels  3.91 us (3%)
    all_to_all x7, blocking collectives, exchange(): lax.all_to_all(x, axes, split_axis=0, concat_axis=0, tiled=True, axis_ind...  116 us

profile of v7, /device:TPU:1, one launch (start us, length us, event | category | flops | bytes accessed | tf_op | source)
XLA Modules:
  0.0 120.6 jit_solution(3457066152725502737)
XLA Ops:
  0.0 0.0 copy-start
  0.0 0.0 copy-start.3
  0.0 0.8 copy-done.3
  0.8 17.9 %all_to_all.35.keys_ref = bf16[32,24,128]{2,1,0:T(8,128)(2,1)S(1)} all-to-all(bf16[32,24,128]{2,1,0:T(8,128)(2,1)S(1)} %shard_map.46), channel_id=1, replica_groups=mesh['zh'=4,'zl'=4,'x'=4,'y'=4,'core'=2] {'x','y','core'}, dimensions={0} | all-to-all | bytes 393216 | tf_op jit(solution)/shard_map/all_to_all | solution.py:278
  18.8 0.0 copy-done
  18.8 0.0 copy-start.2
  18.8 1.0 shard_map.47
  19.8 0.0 copy-start.1
  19.8 11.6 %all_to_all.36.in_ref = bf16[8,104,128]{2,1,0:T(8,128)(2,1)S(1)} all-to-all(bf16[8,104,128]{2,1,0:T(8,128)(2,1)S(1)} %get-tuple-element.7), channel_id=1, replica_groups={{0,1,32,33,64,65,96,97},{128,129,160,161,192,193,224,225},{320,321,352,..., dimensions={0} | all-to-all | bytes 425984 | tf_op jit(solution)/shard_map/all_to_all | solution.py:278
  31.4 0.3 shard_map.48
  31.7 30.7 %all_to_all.37.in_ref = bf16[16,4,1664]{2,1,0:T(4,128)(2,1)S(1)} all-to-all(bf16[16,4,1664]{2,1,0:T(4,128)(2,1)S(1)} %shard_map.48), channel_id=1, replica_groups={{0,128,320,448,8,136,328,456,16,144,336,464,24,152,344,472},{32,160,352..., dimensions={0} | all-to-all | bytes 425984 | tf_op jit(solution)/shard_map/all_to_all | solution.py:278
  62.4 0.3 shard_map.49
  62.7 10.1 %all_to_all.38.in_ref = bf16[16,48,128]{2,1,0:T(8,128)(2,1)S(1)} all-to-all(bf16[16,48,128]{2,1,0:T(8,128)(2,1)S(1)} %shard_map.49), channel_id=1, replica_groups={{0,32,64,96,2,34,66,98,4,36,68,100,6,38,70,102},{128,160,192,224,130,16..., dimensions={0} | all-to-all | bytes 393216 | tf_op jit(solution)/shard_map/all_to_all | solution.py:278
  72.8 0.0 copy-done.2
  72.8 0.0 copy-done.1
  72.8 0.8 shard_map.50
  73.6 12.0 %all_to_all.39.in_ref = bf16[8,96,128]{2,1,0:T(8,128)(2,1)S(1)} all-to-all(bf16[8,96,128]{2,1,0:T(8,128)(2,1)S(1)} %shard_map.50), channel_id=1, replica_groups={{0,1,32,33,64,65,96,97},{128,129,160,161,192,193,224,225},{320,321,352,..., dimensions={0} | all-to-all | bytes 393216 | tf_op jit(solution)/shard_map/all_to_all | solution.py:278
  85.6 20.8 %all_to_all.40.in_ref = bf16[16,48,128]{2,1,0:T(8,128)(2,1)S(1)} all-to-all(bf16[16,48,128]{2,1,0:T(8,128)(2,1)S(1)} %shard_map.51), channel_id=1, replica_groups={{0,128,320,448,2,130,322,450,4,132,324,452,6,134,326,454},{32,160,352,4..., dimensions={0} | all-to-all | bytes 393216 | tf_op jit(solution)/shard_map/all_to_all | solution.py:278
  106.5 12.7 %all_to_all.41.in_ref = bf16[16,48,128]{2,1,0:T(8,128)(2,1)S(1)} all-to-all(bf16[16,48,128]{2,1,0:T(8,128)(2,1)S(1)} %shard_map.52), channel_id=1, replica_groups={{0,32,64,96,8,40,72,104,16,48,80,112,24,56,88,120},{128,160,192,224,136..., dimensions={0} | all-to-all | bytes 393216 | tf_op jit(solution)/shard_map/all_to_all | solution.py:278
  119.2 1.4 %shard_map.53 = bf16[1,224,3072]{2,1,0:T(8,128)(2,1)} custom-call(bf16[16,48,128]{2,1,0:T(8,128)(2,1)S(1)} %all_to_all.41.in_ref, bf16[224,32]{1,0:T(8,128)(2,1)S(1)} %get-tuple-element.8.combine_ref), custom_call_target="tpu_custom_call" | custom-call | tf_op jit(solution)/shard_map/pallas_call | solution.py:333
  (3 shorter events, 0.1 us)
Async XLA Ops:
  0.0 18.8 %copy-start = (bf16[1,224,3072]{2,1,0:T(8,128)(2,1)S(1)}, bf16[1,224,3072]{2,1,0:T(8,128)(2,1)}, u32[]{:S(2)}) copy-start(bf16[1,224,3072]{2,1,0:T(8,128)(2,1)} %patch_ref.3) | copy-start | bytes 4128772
  0.0 0.8 copy-start.3
  18.8 54.0 %copy-start.2 = (bf16[1,192,3072]{2,1,0:T(8,128)(2,1)S(1)}, bf16[1,192,3072]{2,1,0:T(8,128)(2,1)}, u32[]{:S(2)}) copy-start(bf16[1,192,3072]{2,1,0:T(8,128)(2,1)} %second_ref.1) | copy-start | bytes 3538948
  19.8 53.0 %copy-start.1 = (bf16[1,3072,192]{1,2,0:T(8,128)(2,1)S(1)}, bf16[1,3072,192]{1,2,0:T(8,128)(2,1)}, u32[]{:S(2)}) copy-start(bf16[1,3072,192]{1,2,0:T(8,128)(2,1)} %param.6) | copy-start | bytes 3538948

commit v8 on v7

--- a/solution.py
+++ b/solution.py
@@ -279,7 +279,7 @@
 
 
 def column(h, z):
-    return (z + 2 * (h // 2)) % SIDE
+    return (z + 2 * ((h + 1) // 2 % 2)) % SIDE
 
 
 NEAR = [sorted((SIDE * h + z for z in range(SIDE)), key=lambda p: column(p // SIDE, p % SIDE)) for h in range(SIDE)]

time: 121 us -> 120 us (level)
  no operation moved by 1% of the time
where the time goes in v8:
time: 120 us
  blocking collectives  115 us (96%)
  Pallas kernels  3.9 us (3%)
    all_to_all x7, blocking collectives, exchange(): lax.all_to_all(x, axes, split_axis=0, concat_axis=0, tiled=True, axis_ind...  115 us

profile of v8, /device:TPU:1, one launch (start us, length us, event | category | flops | bytes accessed | tf_op | source)
XLA Modules:
  0.0 119.5 jit_solution(14432504736330484818)
XLA Ops:
  0.0 0.0 copy-start
  0.0 0.0 copy-start.3
  0.0 0.8 copy-done.3
  0.8 17.9 %all_to_all.35.keys_ref = bf16[32,24,128]{2,1,0:T(8,128)(2,1)S(1)} all-to-all(bf16[32,24,128]{2,1,0:T(8,128)(2,1)S(1)} %shard_map.46), channel_id=1, replica_groups=mesh['zh'=4,'zl'=4,'x'=4,'y'=4,'core'=2] {'x','y','core'}, dimensions={0} | all-to-all | bytes 393216 | tf_op jit(solution)/shard_map/all_to_all | solution.py:278
  18.8 0.0 copy-done
  18.8 0.0 copy-start.2
  18.8 1.0 shard_map.47
  19.8 0.0 copy-start.1
  19.8 11.6 %all_to_all.36.in_ref = bf16[8,104,128]{2,1,0:T(8,128)(2,1)S(1)} all-to-all(bf16[8,104,128]{2,1,0:T(8,128)(2,1)S(1)} %get-tuple-element.7), channel_id=1, replica_groups={{0,1,32,33,64,65,96,97},{192,193,224,225,128,129,160,161},{320,321,352,..., dimensions={0} | all-to-all | bytes 425984 | tf_op jit(solution)/shard_map/all_to_all | solution.py:278
  31.4 0.3 shard_map.48
  31.7 28.9 %all_to_all.37.in_ref = bf16[16,4,1664]{2,1,0:T(4,128)(2,1)S(1)} all-to-all(bf16[16,4,1664]{2,1,0:T(4,128)(2,1)S(1)} %shard_map.48), channel_id=1, replica_groups={{0,192,320,384,8,200,328,392,16,208,336,400,24,216,344,408},{32,224,352..., dimensions={0} | all-to-all | bytes 425984 | tf_op jit(solution)/shard_map/all_to_all | solution.py:278
  60.6 0.3 shard_map.49
  60.9 12.0 %all_to_all.38.in_ref = bf16[16,48,128]{2,1,0:T(8,128)(2,1)S(1)} all-to-all(bf16[16,48,128]{2,1,0:T(8,128)(2,1)S(1)} %shard_map.49), channel_id=1, replica_groups={{0,32,64,96,2,34,66,98,4,36,68,100,6,38,70,102},{192,224,128,160,194,22..., dimensions={0} | all-to-all | bytes 393216 | tf_op jit(solution)/shard_map/all_to_all | solution.py:278
  73.0 0.0 copy-done.2
  73.0 0.0 copy-done.1
  73.0 0.8 shard_map.50
  73.7 12.0 %all_to_all.39.in_ref = bf16[8,96,128]{2,1,0:T(8,128)(2,1)S(1)} all-to-all(bf16[8,96,128]{2,1,0:T(8,128)(2,1)S(1)} %shard_map.50), channel_id=1, replica_groups={{0,1,32,33,64,65,96,97},{192,193,224,225,128,129,160,161},{320,321,352,..., dimensions={0} | all-to-all | bytes 393216 | tf_op jit(solution)/shard_map/all_to_all | solution.py:278
  85.8 20.9 %all_to_all.40.in_ref = bf16[16,48,128]{2,1,0:T(8,128)(2,1)S(1)} all-to-all(bf16[16,48,128]{2,1,0:T(8,128)(2,1)S(1)} %shard_map.51), channel_id=1, replica_groups={{0,192,320,384,2,194,322,386,4,196,324,388,6,198,326,390},{32,224,352,4..., dimensions={0} | all-to-all | bytes 393216 | tf_op jit(solution)/shard_map/all_to_all | solution.py:278
  106.7 11.5 %all_to_all.41.in_ref = bf16[16,48,128]{2,1,0:T(8,128)(2,1)S(1)} all-to-all(bf16[16,48,128]{2,1,0:T(8,128)(2,1)S(1)} %shard_map.52), channel_id=1, replica_groups={{0,32,64,96,8,40,72,104,16,48,80,112,24,56,88,120},{192,224,128,160,200..., dimensions={0} | all-to-all | bytes 393216 | tf_op jit(solution)/shard_map/all_to_all | solution.py:278
  118.2 1.4 %shard_map.53 = bf16[1,224,3072]{2,1,0:T(8,128)(2,1)} custom-call(bf16[16,48,128]{2,1,0:T(8,128)(2,1)S(1)} %all_to_all.41.in_ref, bf16[224,32]{1,0:T(8,128)(2,1)S(1)} %get-tuple-element.8.combine_ref), custom_call_target="tpu_custom_call" | custom-call | tf_op jit(solution)/shard_map/pallas_call | solution.py:333
  (3 shorter events, 0.1 us)
Async XLA Ops:
  0.0 18.8 %copy-start = (bf16[1,224,3072]{2,1,0:T(8,128)(2,1)S(1)}, bf16[1,224,3072]{2,1,0:T(8,128)(2,1)}, u32[]{:S(2)}) copy-start(bf16[1,224,3072]{2,1,0:T(8,128)(2,1)} %patch_ref.3) | copy-start | bytes 4128772
  0.0 0.8 copy-start.3
  18.8 54.2 %copy-start.2 = (bf16[1,192,3072]{2,1,0:T(8,128)(2,1)S(1)}, bf16[1,192,3072]{2,1,0:T(8,128)(2,1)}, u32[]{:S(2)}) copy-start(bf16[1,192,3072]{2,1,0:T(8,128)(2,1)} %second_ref.1) | copy-start | bytes 3538948
  19.8 53.1 %copy-start.1 = (bf16[1,3072,192]{1,2,0:T(8,128)(2,1)S(1)}, bf16[1,3072,192]{1,2,0:T(8,128)(2,1)}, u32[]{:S(2)}) copy-start(bf16[1,3072,192]{1,2,0:T(8,128)(2,1)} %param.6) | copy-start | bytes 3538948
